TPU v7x, 256 devices: a whole 4x4x8 slice. The times are simulated.
256 devices in a mesh: ctx: 32 (over z, x), head: 8 (over y, core).
Axes of the slice: x: 4, y: 4, z: 8, core: 2. Of those that a mesh axis runs over, the one named last changes fastest.
Arguments:
- queries: bfloat16 [65536, 4096], P(('ctx', 'head')), may hold values from -8 to 8
- new_keys: bfloat16 [65536, 1024], P(('ctx', 'head')), may hold values from -4 to 4
- new_values: bfloat16 [65536, 1024], P(('ctx', 'head')), may hold values from -4 to 4
- cache_keys: bfloat16 [131072, 1024], P('ctx', 'head'), may hold values from -4 to 4
- cache_values: bfloat16 [131072, 1024], P('ctx', 'head'), may hold values from -4 to 4
- chosen: int32 [128, 8, 3], P('ctx', 'head'), may hold values from 0 to 255, as said below
Outputs:
- attended: bfloat16 [65536, 4096], P(('ctx', 'head'))
Inputs may be any that keep to these rules, and one draw needn't show every extreme that they name: `chosen`: for each query block and key-value head the 3 ids are distinct. Cache block j lies on the device of index j // 8 along ctx. For each key-value head, the 4 query blocks of one device along ctx name the blocks of any one device at most 1 times together, and those of some device exactly 1 times.
All inputs are finite; a program needn't handle non-finite values.
Results may differ from a plain program's by a relative error of at most 0.0048.
Values may be sent and summed in bfloat16 or wider, within the bound.
No kernel may reach another device: no remote copies, remote signals or barrier semaphores. Data moves between devices by JAX's collectives and lax.ppermute only.
A program may use at most 192 MiB of HBM per device.

v0:
```python
import math

import jax
import jax.numpy as jnp
from jax import lax
from jax.sharding import PartitionSpec as P

HD = 128
BLK = 512


def make_table(picked, ctx_size, slot_cap, cache_blocks):
    query_blocks, kv_heads, picks_per = picked.shape
    flat = picked.transpose(1, 0, 2).reshape(kv_heads, query_blocks * picks_per)
    owner_ids = flat // cache_blocks
    local_ids = flat % cache_blocks
    request_index = jnp.arange(query_blocks * picks_per)
    earlier = request_index[None, :] < request_index[:, None]
    same_owner = owner_ids[:, :, None] == owner_ids[:, None, :]
    ranks = jnp.sum((same_owner & earlier[None]).astype(jnp.int32), axis=2)
    match = (owner_ids[:, None, None, :] == jnp.arange(ctx_size)[None, :, None, None]) & (
        ranks[:, None, None, :] == jnp.arange(slot_cap)[None, None, :, None]
    )
    table = jnp.sum(jnp.where(match, local_ids[:, None, None, :] + 1, 0), axis=3) - 1
    owner_grid = owner_ids.reshape(kv_heads, query_blocks, picks_per).transpose(1, 0, 2)
    rank_grid = ranks.reshape(kv_heads, query_blocks, picks_per).transpose(1, 0, 2)
    return (table.transpose(1, 0, 2), owner_grid, rank_grid)


def local(queries, new_keys, new_values, cache_keys, cache_values, chosen):
    head_rows, key_rows, value_rows = (
        lax.all_to_all(queries, "head", split_axis=1, concat_axis=0, tiled=True),
        lax.all_to_all(new_keys, "head", split_axis=1, concat_axis=0, tiled=True),
        lax.all_to_all(new_values, "head", split_axis=1, concat_axis=0, tiled=True),
    )
    ctx_size = lax.axis_size("ctx")
    slab_rows = head_rows.shape[0]
    query_blocks = slab_rows // BLK
    kv_heads = key_rows.shape[1] // HD
    group_size = head_rows.shape[1] // (kv_heads * HD)
    cache_blocks = cache_keys.shape[0] // BLK
    picks_per = chosen.shape[2]
    slot_cap = (picks_per * query_blocks + ctx_size - 1) // ctx_size
    score_scale = 1.0 / math.sqrt(HD)
    query_grid = head_rows.reshape(query_blocks, BLK, kv_heads, group_size, HD)
    own_keys = key_rows.reshape(query_blocks, BLK, kv_heads, HD)
    own_values = value_rows.reshape(query_blocks, BLK, kv_heads, HD)
    causal = jnp.arange(BLK)[None, :] <= jnp.arange(BLK)[:, None]

    def own_scores(query_rows, block_keys):
        raw_scores = (
            jnp.einsum("tkgd,skd->kgts", query_rows, block_keys, preferred_element_type=jnp.float32)
            * score_scale
        )
        return jnp.where(causal, raw_scores, -jnp.inf)

    table, owner_grid, rank_grid = make_table(chosen, ctx_size, slot_cap, cache_blocks)
    wanted = lax.all_to_all(table, "ctx", split_axis=0, concat_axis=0, tiled=True)
    store_k = cache_keys.reshape(cache_blocks, BLK, kv_heads, HD).transpose(2, 0, 1, 3)
    store_v = cache_values.reshape(cache_blocks, BLK, kv_heads, HD).transpose(2, 0, 1, 3)
    head_grid = jnp.arange(kv_heads)[None, :, None]
    safe_ids = jnp.maximum(wanted, 0)
    live = (wanted >= 0)[:, :, :, None, None]
    picked_k = jnp.where(live, store_k[head_grid, safe_ids], jnp.zeros((), store_k.dtype))
    picked_v = jnp.where(live, store_v[head_grid, safe_ids], jnp.zeros((), store_v.dtype))

    def arrange(received):
        fetched = received[owner_grid, head_grid, rank_grid]
        return fetched.reshape(query_blocks, kv_heads, picks_per * BLK, HD)

    def near_of(packed_query, packed_near):
        return own_scores(packed_query, packed_near)

    got_k, got_v = (
        lax.all_to_all(picked_k, "ctx", split_axis=0, concat_axis=0, tiled=True),
        lax.all_to_all(picked_v, "ctx", split_axis=0, concat_axis=0, tiled=True),
    )
    far_keys = arrange(got_k)
    far_values = arrange(got_v)

    def attend(packed):
        query_rows, near_in, keys_far, values_far, values_near = packed
        near = near_of(query_rows, near_in)
        far = (
            jnp.einsum("tkgd,ksd->kgts", query_rows, keys_far, preferred_element_type=jnp.float32)
            * score_scale
        )
        scores = jnp.concatenate([far, near], axis=3)
        row_max = jnp.max(scores, axis=3, keepdims=True)
        weights = jnp.exp(scores - row_max)
        totals = jnp.sum(weights, axis=3, keepdims=True)
        weights_bf = weights.astype(jnp.bfloat16)
        values_all = jnp.concatenate([values_far, values_near.transpose(1, 0, 2)], axis=1)
        mixed_out = jnp.einsum(
            "kgts,ksd->tkgd", weights_bf, values_all, preferred_element_type=jnp.float32
        )
        mixed_out = mixed_out / totals.transpose(2, 0, 1, 3)
        return mixed_out.astype(jnp.bfloat16).reshape(BLK, kv_heads * group_size * HD)

    results = lax.map(attend, (query_grid, own_keys, far_keys, far_values, own_values))
    attended = results.reshape(slab_rows, kv_heads * group_size * HD)
    return lax.all_to_all(attended, "head", split_axis=0, concat_axis=1, tiled=True)


def solution(mesh):
    in_specs = (
        P(("ctx", "head"), None),
        P(("ctx", "head"), None),
        P(("ctx", "head"), None),
        P("ctx", "head"),
        P("ctx", "head"),
        P("ctx", "head", None),
    )
    out_specs = P(("ctx", "head"), None)
    return jax.shard_map(local, mesh=mesh, in_specs=in_specs, out_specs=out_specs, check_vma=False)
```

profile of v0, /device:TPU:1, one launch (start us, length us, event | category | flops | bytes accessed | tf_op | source)
XLA Modules:
  0.0 422.1 jit_solution(3371238067762159323)
XLA Ops:
  2.2 11.9 %all-to-all-start = ((s32[32,1,1]{2,1,0:T(1,128)}), s32[32,1,1]{2,1,0:T(1,128)S(1)}, u32[]{:S(2)}, u32[]{:S(2)}) async-start(s32[32,1,1]{2,1,0:T(1,128)} %copy.85), calls=%async_computation | async-start | bytes 32768 | tf_op jit(solution)/shard_map/all_to_all | solution.py:58
  14.1 2.0 copy.91
  16.1 6.5 %all-to-all-done = s32[32,1,1]{2,1,0:T(1,128)S(1)} async-done(((s32[32,1,1]{2,1,0:T(1,128)}), s32[32,1,1]{2,1,0:T(1,128)S(1)}, u32[]{:S(2)}, u32[]{:S(2)}) %all-to-all-start) | async-done | bytes 160 | tf_op jit(solution)/shard_map/all_to_all | solution.py:58
  22.6 6.6 %all-to-all-start.2 = ((bf16[256,8,128]{0,2,1:T(8,128)(2,1)}), bf16[256,8,128]{0,2,1:T(8,128)(2,1)S(1)}, u32[]{:S(2)}, u32[]{:S(2)}) async-start(bf16[256,8,128]{0,2,1:T(8,128)(2,1)} %bitcast.8), calls=%async_computation.2 | async-start | bytes 1048576 | tf_op jit(solution)/shard_map/all_to_all | solution.py:34
  29.1 3.1 copy.119
  32.2 6.4 %all-to-all-done.2 = bf16[256,8,128]{0,2,1:T(8,128)(2,1)S(1)} async-done(((bf16[256,8,128]{0,2,1:T(8,128)(2,1)}), bf16[256,8,128]{0,2,1:T(8,128)(2,1)S(1)}, u32[]{:S(2)}, u32[]{:S(2)}) %all-to-all-start.2) | async-done | bytes 524320 | tf_op jit(solution)/shard_map/all_to_all | solution.py:34
  38.6 5.1 %all-to-all-start.4 = ((bf16[256,8,512]{2,0,1:T(8,128)(2,1)}), bf16[256,8,512]{2,0,1:T(8,128)(2,1)}, u32[]{:S(2)}, u32[]{:S(2)}) async-start(bf16[256,8,512]{2,0,1:T(8,128)(2,1)} %bitcast.96), calls=%async_computation.4 | async-start | bytes 4194304 | tf_op jit(solution)/shard_map/all_to_all | solution.py:32
  44.4 3.0 gather_fusion
  47.5 3.0 gather_fusion.2
  51.2 5.8 %bitcast_select_fusion.1 = (bf16[32,1,1,512,128]{4,3,2,1,0:T(8,128)(2,1)}, bf16[32,1,1,512,128]{4,3,2,1,0:T(8,128)(2,1)}) fusion(bf16[32,512,128]{2,1,0:T(8,128)(2,1)} %gather_fusion.2, pred[32]{0:T(512)(128)(4,1)S(1)} %compare_reduce_fusion, bf16[32,512,128]{2,1,0:T(8,128)(2,1)} %gather_fusion), kind=kLoop, calls=%fused_computation.36 | loop fusion | flops 4194304 | bytes 16777248 | tf_op jit(solution)/shard_map/jit(_where)/select_n | solution.py:64
  57.0 13.2 %all-to-all-done.4 = bf16[256,8,512]{2,0,1:T(8,128)(2,1)} async-done(((bf16[256,8,512]{2,0,1:T(8,128)(2,1)}), bf16[256,8,512]{2,0,1:T(8,128)(2,1)}, u32[]{:S(2)}, u32[]{:S(2)}) %all-to-all-start.4) | async-done | bytes 2097184 | tf_op jit(solution)/shard_map/all_to_all | solution.py:32
  70.2 98.4 %all_to_all.82 = bf16[32,1,1,512,128]{4,3,2,1,0:T(8,128)(2,1)} all-to-all(bf16[32,1,1,512,128]{4,3,2,1,0:T(8,128)(2,1)} %get-tuple-element.119), channel_id=1, replica_groups=mesh['ctx'=32,'head'=8] {'ctx'}, dimensions={0} | all-to-all | bytes 8388608 | tf_op jit(solution)/shard_map/all_to_all | solution.py:75
  168.6 7.2 %all-to-all-start.1 = ((bf16[32,1,1,512,128]{4,3,2,1,0:T(8,128)(2,1)}), bf16[32,1,1,512,128]{4,3,2,1,0:T(8,128)(2,1)}, u32[]{:S(2)}, u32[]{:S(2)}) async-start(bf16[32,1,1,512,128]{4,3,2,1,0:T(8,128)(2,1)} %get-tuple-element.120), calls=%async_computation.1 | async-start | bytes 8388608 | tf_op jit(solution)/shard_map/all_to_all | solution.py:76
  176.9 90.9 %all-to-all-done.1 = bf16[32,1,1,512,128]{4,3,2,1,0:T(8,128)(2,1)} async-done(((bf16[32,1,1,512,128]{4,3,2,1,0:T(8,128)(2,1)}), bf16[32,1,1,512,128]{4,3,2,1,0:T(8,128)(2,1)}, u32[]{:S(2)}, u32[]{:S(2)}) %all-to-all-start.1) | async-done | bytes 4194336 | tf_op jit(solution)/shard_map/all_to_all | solution.py:76
  267.8 7.3 %all-to-all-start.5 = ((bf16[256,8,128]{2,0,1:T(8,128)(2,1)}), bf16[256,8,128]{2,0,1:T(8,128)(2,1)}, u32[]{:S(2)}, u32[]{:S(2)}) async-start(bf16[256,8,128]{2,0,1:T(8,128)(2,1)} %copy_bitcast_fusion.4), calls=%async_computation.5 | async-start | bytes 1048576 | tf_op jit(solution)/shard_map/all_to_all | solution.py:33
  275.5 1.0 copy.92
  276.5 2.5 reshape.563
  279.0 4.2 gather_fusion.3
  283.2 4.2 gather_fusion.1
  287.4 97.0 %while.11 = (s32[]{:T(128)}, bf16[4,512,512]{2,1,0:T(8,128)(2,1)}, bf16[4,1,1536,128]{3,2,0,1:T(8,128)(2,1)}, bf16[4,512,1,128]{3,1,0,2:T(8,128)(2,1)}, bf16[4,1...) while((s32[]{:T(128)}, bf16[4,512,512]{2,1,0:T(8,128)(2,1)}, ...), condition=%wide.region_6.7_spmd.clone, body=%wide.region_2.6_spmd.clone.sunk | while | flops 2187063296 | bytes 130098864 | solution.py:100
  287.6 3.1 fusion.42
  290.8 1.8 fusion.41
  292.6 5.7 %multiply_bitcast_fusion.3 = (f32[1,4,512,1536]{2,3,1,0:T(8,128)S(1)}, f32[4,512,1536]{1,2,0:T(8,128)}) fusion(f32[1536,512,4]{1,0,2:T(8,128)S(1)} %get-tuple-element.173), kind=kLoop, calls=%fused_computation.12.clone.2 | loop fusion | flops 3145728 | bytes 37748736 | tf_op jit(solution)/shard_map/while/body/eval_jaxpr/mul | solution.py:85
  298.3 2.3 fusion.43
  300.7 1.0 constant_dynamic-slice_fusion.8
  301.9 0.9 constant_dynamic-slice_fusion.7
  302.9 7.6 %divide_convert_fusion.2 = bf16[512,1,4,128]{0,3,2,1:T(8,128)(2,1)S(1)} fusion(f32[4,512,512]{1,2,0:T(8,128)} %bitcast.124, f32[4,512,1536]{1,2,0:T(8,128)} %get-tuple-element.174, f32[4,512]{1,0:T(4,128)S(1)} %reduce_max.30, bf16[1,512,128]{1,2,0:T(8,128)(2,1)S(1)} %bitcast.132, bf16[1,1536,128]{1,2,0:T(8,128)(2,1)S(1)} %bitcast.127, ...), kind=kOutput, calls=%fused_computation.17.clone.1 | convolution fusion | flops 1087897600 | bytes 17842176 | tf_op jit(solution)/shard_map/while/body/eval_jaxpr/kgts,ksd->tkgd/dot_general | solution.py:94
  311.8 3.1 fusion.42
  315.0 1.8 fusion.41
  316.9 5.7 %multiply_bitcast_fusion.3 = (f32[1,4,512,1536]{2,3,1,0:T(8,128)S(1)}, f32[4,512,1536]{1,2,0:T(8,128)}) fusion(f32[1536,512,4]{1,0,2:T(8,128)S(1)} %get-tuple-element.173), kind=kLoop, calls=%fused_computation.12.clone.2 | loop fusion | flops 3145728 | bytes 37748736 | tf_op jit(solution)/shard_map/while/body/eval_jaxpr/mul | solution.py:85
  322.6 2.3 fusion.43
  324.9 1.0 constant_dynamic-slice_fusion.8
  327.2 7.6 %divide_convert_fusion.2 = bf16[512,1,4,128]{0,3,2,1:T(8,128)(2,1)S(1)} fusion(f32[4,512,512]{1,2,0:T(8,128)} %bitcast.124, f32[4,512,1536]{1,2,0:T(8,128)} %get-tuple-element.174, f32[4,512]{1,0:T(4,128)S(1)} %reduce_max.30, bf16[1,512,128]{1,2,0:T(8,128)(2,1)S(1)} %bitcast.132, bf16[1,1536,128]{1,2,0:T(8,128)(2,1)S(1)} %bitcast.127, ...), kind=kOutput, calls=%fused_computation.17.clone.1 | convolution fusion | flops 1087897600 | bytes 17842176 | tf_op jit(solution)/shard_map/while/body/eval_jaxpr/kgts,ksd->tkgd/dot_general | solution.py:94
  336.1 3.1 fusion.42
  339.3 1.8 fusion.41
  341.1 5.7 %multiply_bitcast_fusion.3 = (f32[1,4,512,1536]{2,3,1,0:T(8,128)S(1)}, f32[4,512,1536]{1,2,0:T(8,128)}) fusion(f32[1536,512,4]{1,0,2:T(8,128)S(1)} %get-tuple-element.173), kind=kLoop, calls=%fused_computation.12.clone.2 | loop fusion | flops 3145728 | bytes 37748736 | tf_op jit(solution)/shard_map/while/body/eval_jaxpr/mul | solution.py:85
  346.9 2.3 fusion.43
  349.2 1.0 constant_dynamic-slice_fusion.8
  351.5 7.6 %divide_convert_fusion.2 = bf16[512,1,4,128]{0,3,2,1:T(8,128)(2,1)S(1)} fusion(f32[4,512,512]{1,2,0:T(8,128)} %bitcast.124, f32[4,512,1536]{1,2,0:T(8,128)} %get-tuple-element.174, f32[4,512]{1,0:T(4,128)S(1)} %reduce_max.30, bf16[1,512,128]{1,2,0:T(8,128)(2,1)S(1)} %bitcast.132, bf16[1,1536,128]{1,2,0:T(8,128)(2,1)S(1)} %bitcast.127, ...), kind=kOutput, calls=%fused_computation.17.clone.1 | convolution fusion | flops 1087897600 | bytes 17842176 | tf_op jit(solution)/shard_map/while/body/eval_jaxpr/kgts,ksd->tkgd/dot_general | solution.py:94
  360.3 3.1 fusion.42
  363.6 1.8 fusion.41
  365.4 5.7 %multiply_bitcast_fusion.3 = (f32[1,4,512,1536]{2,3,1,0:T(8,128)S(1)}, f32[4,512,1536]{1,2,0:T(8,128)}) fusion(f32[1536,512,4]{1,0,2:T(8,128)S(1)} %get-tuple-element.173), kind=kLoop, calls=%fused_computation.12.clone.2 | loop fusion | flops 3145728 | bytes 37748736 | tf_op jit(solution)/shard_map/while/body/eval_jaxpr/mul | solution.py:85
  371.1 2.3 fusion.43
  373.4 1.0 constant_dynamic-slice_fusion.8
  375.7 7.6 %divide_convert_fusion.2 = bf16[512,1,4,128]{0,3,2,1:T(8,128)(2,1)S(1)} fusion(f32[4,512,512]{1,2,0:T(8,128)} %bitcast.124, f32[4,512,1536]{1,2,0:T(8,128)} %get-tuple-element.174, f32[4,512]{1,0:T(4,128)S(1)} %reduce_max.30, bf16[1,512,128]{1,2,0:T(8,128)(2,1)S(1)} %bitcast.132, bf16[1,1536,128]{1,2,0:T(8,128)(2,1)S(1)} %bitcast.127, ...), kind=kOutput, calls=%fused_computation.17.clone.1 | convolution fusion | flops 1087897600 | bytes 17842176 | tf_op jit(solution)/shard_map/while/body/eval_jaxpr/kgts,ksd->tkgd/dot_general | solution.py:94
  384.4 31.3 %all_to_all.83 = bf16[8,256,512]{2,1,0:T(8,128)(2,1)S(1)} all-to-all(bf16[8,256,512]{2,1,0:T(8,128)(2,1)} %bitcast.135), channel_id=1, replica_groups=mesh['ctx'=32,'head'=8] {'head'}, dimensions={0} | all-to-all | bytes 4194304 | tf_op jit(solution)/shard_map/all_to_all | solution.py:102
  415.7 2.4 copy.100
  418.1 4.1 copy.101
  (90 shorter events, 14.3 us)
Async XLA Ops:
  0.0 44.4 %copy-start = (bf16[4096,128]{1,0:T(8,128)(2,1)S(1)}, bf16[4096,128]{1,0:T(8,128)(2,1)}, u32[]{:S(2)}) copy-start(bf16[4096,128]{1,0:T(8,128)(2,1)} %param.12) | copy-start | bytes 3145732
  2.2 20.4 %all-to-all-start = ((s32[32,1,1]{2,1,0:T(1,128)}), s32[32,1,1]{2,1,0:T(1,128)S(1)}, u32[]{:S(2)}, u32[]{:S(2)}) async-start(s32[32,1,1]{2,1,0:T(1,128)} %copy.85), calls=%async_computation | async-start | bytes 32768 | tf_op jit(solution)/shard_map/all_to_all | solution.py:58
  22.6 16.1 %all-to-all-start.2 = ((bf16[256,8,128]{0,2,1:T(8,128)(2,1)}), bf16[256,8,128]{0,2,1:T(8,128)(2,1)S(1)}, u32[]{:S(2)}, u32[]{:S(2)}) async-start(bf16[256,8,128]{0,2,1:T(8,128)(2,1)} %bitcast.8), calls=%async_computation.2 | async-start | bytes 1048576 | tf_op jit(solution)/shard_map/all_to_all | solution.py:34
  38.6 31.6 %all-to-all-start.4 = ((bf16[256,8,512]{2,0,1:T(8,128)(2,1)}), bf16[256,8,512]{2,0,1:T(8,128)(2,1)}, u32[]{:S(2)}, u32[]{:S(2)}) async-start(bf16[256,8,512]{2,0,1:T(8,128)(2,1)} %bitcast.96), calls=%async_computation.4 | async-start | bytes 4194304 | tf_op jit(solution)/shard_map/all_to_all | solution.py:32
  44.4 3.0 copy-start.3
  168.5 7.4 %copy-start.7 = (s32[4,1,3]{0,1,2:T(1,128)S(1)}, s32[4,1,3]{0,1,2:T(1,128)}, u32[]{:S(2)}) copy-start(s32[4,1,3]{0,1,2:T(1,128)} %param.13) | copy-start | bytes 148
  168.6 7.4 %copy-start.6 = (bf16[256,1024]{1,0:T(8,128)(2,1)S(1)}, bf16[256,1024]{1,0:T(8,128)(2,1)}, u32[]{:S(2)}) copy-start(bf16[256,1024]{1,0:T(8,128)(2,1)} %param.9) | copy-start | bytes 1572868
  168.6 99.2 %all-to-all-start.1 = ((bf16[32,1,1,512,128]{4,3,2,1,0:T(8,128)(2,1)}), bf16[32,1,1,512,128]{4,3,2,1,0:T(8,128)(2,1)}, u32[]{:S(2)}, u32[]{:S(2)}) async-start(bf16[32,1,1,512,128]{4,3,2,1,0:T(8,128)(2,1)} %get-tuple-element.120), calls=%async_computation.1 | async-start | bytes 8388608 | tf_op jit(solution)/shard_map/all_to_all | solution.py:76
  267.8 19.6 %all-to-all-start.5 = ((bf16[256,8,128]{2,0,1:T(8,128)(2,1)}), bf16[256,8,128]{2,0,1:T(8,128)(2,1)}, u32[]{:S(2)}, u32[]{:S(2)}) async-start(bf16[256,8,128]{2,0,1:T(8,128)(2,1)} %copy_bitcast_fusion.4), calls=%async_computation.5 | async-start | bytes 1048576 | tf_op jit(solution)/shard_map/all_to_all | solution.py:33
  287.4 3.3 copy-start.4
  292.6 5.8 %copy-start.2 = (f32[1,4,512,512]{2,3,1,0:T(8,128)}, f32[1,4,512,512]{2,3,1,0:T(8,128)S(1)}, u32[]{:S(2)}) copy-start(f32[1,4,512,512]{2,3,1,0:T(8,128)S(1)} %get-tuple-element.172) | copy-start | bytes 12582916 | tf_op jit(solution)/shard_map/while
  302.9 8.7 %copy-start.5 = (bf16[4,512,1,4,128]{4,3,1,0,2:T(4,128)(2,1)S(1)}, bf16[4,512,1,4,128]{4,3,1,0,2:T(4,128)(2,1)}, u32[]{:S(2)}) copy-start(bf16[4,512,1,4,128]{4,3,1,0,2:T(4,128)(2,1)} %copy-done.4) | copy-start | bytes 6291460 | tf_op jit(solution)/shard_map/while
  311.6 3.3 copy-start.4
  316.8 5.8 %copy-start.2 = (f32[1,4,512,512]{2,3,1,0:T(8,128)}, f32[1,4,512,512]{2,3,1,0:T(8,128)S(1)}, u32[]{:S(2)}) copy-start(f32[1,4,512,512]{2,3,1,0:T(8,128)S(1)} %get-tuple-element.172) | copy-start | bytes 12582916 | tf_op jit(solution)/shard_map/while
  327.2 8.7 %copy-start.5 = (bf16[4,512,1,4,128]{4,3,1,0,2:T(4,128)(2,1)S(1)}, bf16[4,512,1,4,128]{4,3,1,0,2:T(4,128)(2,1)}, u32[]{:S(2)}) copy-start(bf16[4,512,1,4,128]{4,3,1,0,2:T(4,128)(2,1)} %copy-done.4) | copy-start | bytes 6291460 | tf_op jit(solution)/shard_map/while
  335.9 3.3 copy-start.4
  341.1 5.8 %copy-start.2 = (f32[1,4,512,512]{2,3,1,0:T(8,128)}, f32[1,4,512,512]{2,3,1,0:T(8,128)S(1)}, u32[]{:S(2)}) copy-start(f32[1,4,512,512]{2,3,1,0:T(8,128)S(1)} %get-tuple-element.172) | copy-start | bytes 12582916 | tf_op jit(solution)/shard_map/while
  351.4 8.7 %copy-start.5 = (bf16[4,512,1,4,128]{4,3,1,0,2:T(4,128)(2,1)S(1)}, bf16[4,512,1,4,128]{4,3,1,0,2:T(4,128)(2,1)}, u32[]{:S(2)}) copy-start(bf16[4,512,1,4,128]{4,3,1,0,2:T(4,128)(2,1)} %copy-done.4) | copy-start | bytes 6291460 | tf_op jit(solution)/shard_map/while
  360.2 3.3 copy-start.4
  365.4 5.8 %copy-start.2 = (f32[1,4,512,512]{2,3,1,0:T(8,128)}, f32[1,4,512,512]{2,3,1,0:T(8,128)S(1)}, u32[]{:S(2)}) copy-start(f32[1,4,512,512]{2,3,1,0:T(8,128)S(1)} %get-tuple-element.172) | copy-start | bytes 12582916 | tf_op jit(solution)/shard_map/while
  375.7 8.7 %copy-start.5 = (bf16[4,512,1,4,128]{4,3,1,0,2:T(4,128)(2,1)S(1)}, bf16[4,512,1,4,128]{4,3,1,0,2:T(4,128)(2,1)}, u32[]{:S(2)}) copy-start(bf16[4,512,1,4,128]{4,3,1,0,2:T(4,128)(2,1)} %copy-done.4) | copy-start | bytes 6291460 | tf_op jit(solution)/shard_map/while
  415.7 6.4 %copy-start.1 = (bf16[4096,128]{1,0:T(8,128)(2,1)S(1)}, bf16[4096,128]{1,0:T(8,128)(2,1)}, u32[]{:S(2)}) copy-start(bf16[4096,128]{1,0:T(8,128)(2,1)} %param.12) | copy-start | bytes 3145732
where the time goes:
time: 423 us; the launch traced here: 422 us
  blocking collectives  130 us (31%)
  waiting for transfers between devices  117 us (28%)
  matrix products  50.2 us (12%)
  local copies, waits for them, and re-layouts  46.5 us (11%)
  other arithmetic  40.4 us (10%)
  starting transfers between devices  38 us (9%)
    all_to_all x1, blocking collectives, local(): lax.all_to_all(picked_k, 'ctx', split_axis=0, concat_axis=0, tiled=True)  98.4 us
    all_to_all x1, waiting for transfers between devices, local(): lax.all_to_all(picked_v, 'ctx', split_axis=0, concat_axis=0, tiled=True)  90.9 us
    all_to_all x1, blocking collectives, local(): lax.all_to_all(attended, 'head', split_axis=0, concat_axis=1, tiled=True)  31.3 us
    dot_general x4, matrix products, attend(): jnp.einsum('kgts,ksd->tkgd', weights_bf, values_all, preferred_element_ty...  30.5 us
    mul x4, other arithmetic, attend(): jnp.einsum('tkgd,ksd->kgts', query_rows, keys_far, preferred_element_type...  23 us
    all_to_all x1, waiting for transfers between devices, local(): lax.all_to_all(queries, 'head', split_axis=1, concat_axis=0, tiled=True)  13.2 us
    dot_general x4, matrix products, attend(): jnp.einsum('tkgd,ksd->kgts', query_rows, keys_far, preferred_element_type...  12.5 us
    all_to_all x1, starting transfers between devices, local(): lax.all_to_all(table, 'ctx', split_axis=0, concat_axis=0, tiled=True)  11.9 us
  transfers between devices with their start and end apart: 5, of which 4 were waited for; matrix products, arithmetic and copies ran while one was open for 8% of the time, Pallas kernels for 0%

commit v1 on v0

v1 whole, which is shorter than its diff:
```python
import functools
import math

import jax
import jax.numpy as jnp
from jax import lax
from jax.experimental import pallas as pl
from jax.experimental.pallas import tpu as pltpu
from jax.sharding import Mesh
from jax.sharding import PartitionSpec as P

HD = 128
BLK = 512
EXP_SCALE = math.log2(math.e) / math.sqrt(HD)
NEG = -1e30
NT = (((1,), (1,)), ((), ()))
NN = (((1,), (0,)), ((), ()))


def spread_kernel(k_ref, v_ref, o_ref):
    o_ref[:, 0] = jnp.swapaxes(k_ref[...], 0, 1)
    o_ref[:, 1] = jnp.swapaxes(v_ref[...], 0, 1)


def spread(cache_keys, cache_values, pieces):
    blocks = cache_keys.shape[0] // BLK
    rows = BLK // pieces
    step = 8
    shape = (blocks, pieces, rows, HD)
    block = pl.BlockSpec((blocks, step, rows, HD), lambda i: (0, i, 0, 0))
    return pl.pallas_call(
        spread_kernel,
        grid=(pieces // step,),
        in_specs=[block, block],
        out_specs=pl.BlockSpec((step, 2, blocks, rows, HD), lambda i: (i, 0, 0, 0, 0)),
        out_shape=jax.ShapeDtypeStruct((pieces, 2, blocks, rows, HD), cache_keys.dtype),
        name="spread",
    )(cache_keys.reshape(shape), cache_values.reshape(shape))


def pick_kernel(ids_ref, held_ref, o_ref, *, step, picks, blocks):
    first = pl.program_id(0) * step

    def one(i, carry):
        for j in range(picks):
            block_id = ids_ref[(first + i) * picks + j]
            src = block_id // blocks
            at = block_id % blocks
            o_ref[i, 0, j] = held_ref[src, 0, at]
            o_ref[i, 1, j] = held_ref[src, 1, at]
        return carry

    lax.fori_loop(0, step, one, 0, unroll=4)


def pick(ids, held, picks):
    sources, _, blocks, rows, _ = held.shape
    query_blocks = ids.shape[0] // picks
    step = 16
    return pl.pallas_call(
        functools.partial(pick_kernel, step=step, picks=picks, blocks=blocks),
        grid_spec=pltpu.PrefetchScalarGridSpec(
            num_scalar_prefetch=1,
            grid=(query_blocks // step,),
            in_specs=[pl.BlockSpec(held.shape, lambda i, ids: (0, 0, 0, 0, 0))],
            out_specs=pl.BlockSpec((step, 2, picks, rows, HD), lambda i, ids: (i, 0, 0, 0, 0)),
        ),
        out_shape=jax.ShapeDtypeStruct((query_blocks, 2, picks, rows, HD), held.dtype),
        name="pick",
    )(ids, held)


def near_kernel(core_ref, q_ref, k_ref, v_ref, acc_ref, stat_ref, *, group):
    rows = q_ref.shape[0]
    keys = k_ref[...]
    values = v_ref[...]
    q_at = core_ref[0] * rows + lax.broadcasted_iota(jnp.int32, (rows, BLK), 0)
    seen = lax.broadcasted_iota(jnp.int32, (rows, BLK), 1) <= q_at
    for g in range(group):
        cols = slice(g * HD, (g + 1) * HD)
        raw = lax.dot_general(q_ref[:, cols], keys, NT, preferred_element_type=jnp.float32)
        raw = jnp.where(seen, raw, NEG)
        top = jnp.max(raw, axis=1, keepdims=True)
        weights = jnp.where(seen, jnp.exp2((raw - top) * EXP_SCALE), 0.0)
        total = jnp.sum(weights, axis=1, keepdims=True)
        acc_ref[:, cols] = lax.dot_general(
            weights.astype(jnp.bfloat16), values, NN, preferred_element_type=jnp.float32
        )
        stat_ref[0, :, 2 * g : 2 * g + 1] = top
        stat_ref[0, :, 2 * g + 1 : 2 * g + 2] = total


def near_part(core, queries, keys, values):
    rows, width = queries.shape
    heads = keys.shape[1] // HD
    group = width // (heads * HD)
    return pl.pallas_call(
        functools.partial(near_kernel, group=group),
        grid_spec=pltpu.PrefetchScalarGridSpec(
            num_scalar_prefetch=1,
            grid=(heads,),
            in_specs=[
                pl.BlockSpec((rows, group * HD), lambda h, core: (0, h)),
                pl.BlockSpec((BLK, HD), lambda h, core: (0, h)),
                pl.BlockSpec((BLK, HD), lambda h, core: (0, h)),
            ],
            out_specs=[
                pl.BlockSpec((rows, group * HD), lambda h, core: (0, h)),
                pl.BlockSpec((1, rows, 2 * group), lambda h, core: (h, 0, 0)),
            ],
        ),
        out_shape=[
            jax.ShapeDtypeStruct((rows, width), jnp.float32),
            jax.ShapeDtypeStruct((heads, rows, 2 * group), jnp.float32),
        ],
        cost_estimate=pl.CostEstimate(
            flops=4 * rows * BLK * width, bytes_accessed=9 * rows * width, transcendentals=rows * BLK * width // HD
        ),
        name="near",
    )(core, queries, keys, values)


def far_kernel(core_ref, q_ref, kv_ref, acc_ref, stat_ref, *rest, group):
    o_ref = rest[-1]
    pieces, _, _, picks, piece_rows, _ = kv_ref.shape
    far = pieces * picks * piece_rows
    keys = kv_ref[:, 0, 0].reshape(far, HD)
    values = kv_ref[:, 0, 1].reshape(far, HD)
    for g in range(group):
        cols = slice(g * HD, (g + 1) * HD)
        near_top = stat_ref[0, :, 2 * g : 2 * g + 1]
        near_total = stat_ref[0, :, 2 * g + 1 : 2 * g + 2]
        raw = lax.dot_general(q_ref[:, cols], keys, NT, preferred_element_type=jnp.float32)
        top = jnp.maximum(jnp.max(raw, axis=1, keepdims=True), near_top)
        weights = jnp.exp2((raw - top) * EXP_SCALE)
        keep = jnp.exp2((near_top - top) * EXP_SCALE)
        total = jnp.sum(weights, axis=1, keepdims=True) + keep * near_total
        mixed = lax.dot_general(weights.astype(jnp.bfloat16), values, NN, preferred_element_type=jnp.float32)
        mixed = (mixed + keep * acc_ref[:, cols]) / total
        o_ref[:, cols] = mixed.astype(o_ref.dtype)


def far_part(parity, queries, kv, acc, stat, prior):
    rows, width = queries.shape
    pieces, ys, _, picks, piece_rows, _ = kv.shape
    heads = stat.shape[0]
    group = stat.shape[2] // 2
    per = heads // ys
    strip = pl.BlockSpec((rows, group * HD), lambda y, parity: (0, per * y + parity[0]))
    in_specs = [
        strip,
        pl.BlockSpec((pieces, 1, 2, picks, piece_rows, HD), lambda y, parity: (0, y, 0, 0, 0, 0)),
        strip,
        pl.BlockSpec((1, rows, 2 * group), lambda y, parity: (per * y + parity[0], 0, 0)),
    ]
    operands = [parity, queries, kv, acc, stat]
    aliases = {}
    if prior is not None:
        in_specs.append(pl.BlockSpec(memory_space=pl.ANY))
        operands.append(prior)
        aliases = {5: 0}
    far = pieces * picks * piece_rows
    return pl.pallas_call(
        functools.partial(far_kernel, group=group),
        grid_spec=pltpu.PrefetchScalarGridSpec(
            num_scalar_prefetch=1, grid=(ys,), in_specs=in_specs, out_specs=strip
        ),
        out_shape=jax.ShapeDtypeStruct((rows, width), queries.dtype),
        input_output_aliases=aliases,
        cost_estimate=pl.CostEstimate(
            flops=4 * rows * far * width // per,
            bytes_accessed=4 * rows * width + kv.size * 2,
            transcendentals=rows * far * width // HD // per,
        ),
        compiler_params=pltpu.CompilerParams(vmem_limit_bytes=48 * 1024 * 1024),
        name="far",
    )(*operands)


def local(queries, new_keys, new_values, cache_keys, cache_values, chosen):
    ctx_size = lax.axis_size("ctx")
    ys = lax.axis_size("y")
    core = lax.axis_index("core").astype(jnp.int32)
    picks = chosen.shape[2]

    outgoing = spread(cache_keys, cache_values, ctx_size)
    held = lax.all_to_all(outgoing, "ctx", split_axis=0, concat_axis=0, tiled=True)
    ids = lax.all_gather(chosen.reshape(-1), "ctx", tiled=True)

    swap = [(0, 1), (1, 0)]
    mine = jnp.concatenate([new_keys, new_values], axis=1)
    theirs = lax.ppermute(mine, "core", swap)
    both = jnp.where(core == 0, jnp.concatenate([mine, theirs]), jnp.concatenate([theirs, mine]))
    width = new_keys.shape[1]
    acc, stat = near_part(core.reshape(1), queries, both[:, :width], both[:, width:])

    chosen_pieces = pick(ids, held, picks)
    got = lax.all_to_all(chosen_pieces, ("ctx", "y"), split_axis=0, concat_axis=0, tiled=True)
    other = lax.ppermute(got, "core", swap)
    split = (ctx_size, ys) + got.shape[1:]
    out = far_part(core.reshape(1), queries, got.reshape(split), acc, stat, None)
    return far_part((1 - core).reshape(1), queries, other.reshape(split), acc, stat, out)


def solution(mesh):
    ctx_size, head_size = mesh.devices.shape
    fine = Mesh(mesh.devices.reshape(ctx_size, head_size // 2, 2), ("ctx", "y", "core"))
    rows = P(("ctx", "y", "core"), None)
    in_specs = (
        rows,
        rows,
        rows,
        P("ctx", ("y", "core")),
        P("ctx", ("y", "core")),
        P("ctx", ("y", "core"), None),
    )
    return jax.shard_map(local, mesh=fine, in_specs=in_specs, out_specs=rows, check_vma=False)
```

time: 423 us -> 221 us (0.52)
  waiting for transfers between devices: 117 us -> 6.4 us
  Pallas kernels: 0 us -> 55.8 us
  matrix products: 50.2 us -> 0 us
  local copies, waits for them, and re-layouts: 46.5 us -> 5.19 us
  other arithmetic: 40.4 us -> 0.97 us
  starting transfers between devices: 38 us -> 18.4 us
    all_to_all x5 -> x1, waiting for transfers between devices: 117 us -> 0.01 us  [local(): lax.all_to_all(outgoing, 'ctx', split_axis=0, concat_axis=0, tiled=True)]
    pallas_call x0 -> x5, Pallas kernels: none -> 55.8 us  [the longest x2 31.4 us: far_part(): pl.pallas_call(functools.partial(far_kernel, group=group), grid_spec=pltp...]
    unnamed x0 -> x1, blocking collectives: none -> 51.1 us
    dot_general x12 -> x0, matrix products: 50.2 us -> none  [the longest x4 30.5 us: attend(): jnp.einsum('kgts,ksd->tkgd', weights_bf, values_all, preferred_element_ty...]
    all_to_all x2 -> x1, blocking collectives: 130 us -> 82 us  [local(): lax.all_to_all(chosen_pieces, ('ctx', 'y'), split_axis=0, concat_axis=0,...]
    all_to_all x5 -> x1, starting transfers between devices: 38 us -> 12 us  [local(): lax.all_to_all(outgoing, 'ctx', split_axis=0, concat_axis=0, tiled=True)]
    mul x4 -> x0, other arithmetic: 23 us -> none  [attend(): jnp.einsum('tkgd,ksd->kgts', query_rows, keys_far, preferred_element_type...]
    gather x4 -> x0, local copies, waits for them, and re-layouts: 14.4 us -> none  [the longest x2 8.32 us: arrange(): fetched = received[owner_grid, head_grid, rank_grid]]
  transfers between devices with their start and end apart: 5 -> 3, of which waited for: 4 -> 1; matrix products, arithmetic and copies ran while one was open for 8% -> 2% of each run, Pallas kernels for 0% -> 13%
where the time goes in v1:
time: 221 us
  blocking collectives  133 us (60%)
  Pallas kernels  55.8 us (25%)
  starting transfers between devices  18.4 us (8%)
  waiting for transfers between devices  6.4 us (3%)
  local copies, waits for them, and re-layouts  5.19 us (2%)
    all_to_all x1, blocking collectives, local(): lax.all_to_all(chosen_pieces, ('ctx', 'y'), split_axis=0, concat_axis=0,...  82 us
    unnamed x1, blocking collectives  51.1 us
    pallas_call x2, Pallas kernels, far_part(): pl.pallas_call(functools.partial(far_kernel, group=group), grid_spec=pltp...  31.4 us
    pallas_call x1, Pallas kernels, near_part(): pl.pallas_call(functools.partial(near_kernel, group=group), grid_spec=plt...  13.7 us
    all_to_all x1, starting transfers between devices, local(): lax.all_to_all(outgoing, 'ctx', split_axis=0, concat_axis=0, tiled=True)  12 us
    pallas_call x1, Pallas kernels, pick(): pl.pallas_call(functools.partial(pick_kernel, step=step, picks=picks, blo...  6.97 us
    ppermute x1, waiting for transfers between devices, local(): theirs = lax.ppermute(mine, 'core', swap)  6.4 us
    ppermute x1, starting transfers between devices, local(): other = lax.ppermute(got, 'core', swap)  6.14 us
  transfers between devices with their start and end apart: 3, of which 1 were waited for; matrix products, arithmetic and copies ran while one was open for 2% of the time, Pallas kernels for 13%

profile of v1, /device:TPU:1, one launch (start us, length us, event | category | flops | bytes accessed | tf_op | source)
XLA Modules:
  0.0 220.6 jit_solution(5981434612366125149)
XLA Ops:
  0.0 3.8 %spread.1 = bf16[32,2,8,16,128]{4,3,2,1,0:T(8,128)(2,1)} custom-call(bf16[8,32,16,128]{3,2,1,0:T(8,128)(2,1)} %bitcast.9, bf16[8,32,16,128]{3,2,1,0:T(8,128)(2,1)} %bitcast.10), custom_call_target="tpu_custom_call" | custom-call | tf_op jit(solution)/shard_map/spread/pallas_call | solution.py:31
  3.8 0.0 copy-start.5
  3.8 0.0 copy-start.6
  3.8 12.0 %all-to-all-start = ((bf16[32,2,8,16,128]{4,3,2,1,0:T(8,128)(2,1)}), bf16[32,2,8,16,128]{4,3,2,1,0:T(8,128)(2,1)S(1)}, u32[]{:S(2)}, u32[]{:S(2)}) async-start(bf16[32,2,8,16,128]{4,3,2,1,0:T(8,128)(2,1)} %spread.1), calls=%async_computation | async-start | bytes 4194304 | tf_op jit(solution)/shard_map/all_to_all | solution.py:187
  15.8 0.0 copy-done.5
  15.8 0.1 copy.9
  15.9 0.1 reshape.29
  16.0 0.0 copy-done.6
  16.0 0.6 dynamic-slice
  17.2 0.2 dynamic-update-slice
  17.5 51.1 %all-reduce.ids_ref = s32[384]{0:T(512)} all-reduce(s32[384]{0:T(512)S(1)} %dynamic-update-slice), channel_id=1, replica_groups=mesh['ctx'=32,'y'=4,'core'=2] {'ctx'}, use_global_device_ids=true, to_apply=%add | all-reduce | flops 384 | bytes 3072
  68.6 0.0 all-to-all-done.held_ref
  68.6 0.0 copy-start.2
  68.6 1.3 copy-done.2
  69.9 7.0 %pick.1 = bf16[128,2,3,16,128]{4,3,2,1,0:T(8,128)(2,1)} custom-call(s32[384]{0:T(512)} %all-reduce.ids_ref, bf16[32,2,8,16,128]{4,3,2,1,0:T(8,128)(2,1)} %copy-done.2), custom_call_target="tpu_custom_call" | custom-call | tf_op jit(solution)/shard_map/pick/pallas_call | solution.py:60
  76.9 0.0 copy-start.3
  76.9 0.0 copy-start.4
  76.9 82.0 %all_to_all.10 = bf16[128,2,3,16,128]{4,3,2,1,0:T(8,128)(2,1)} all-to-all(bf16[128,2,3,16,128]{4,3,2,1,0:T(8,128)(2,1)} %pick.1), channel_id=1, replica_groups=mesh['ctx'=32,'y'=4,'core'=2] {'ctx','y'}, dimensions={0} | all-to-all | bytes 6291456 | tf_op jit(solution)/shard_map/all_to_all | solution.py:198
  158.9 6.1 %collective-permute-start = (bf16[128,2,3,16,128]{4,3,2,1,0:T(8,128)(2,1)}, bf16[128,2,3,16,128]{4,3,2,1,0:T(8,128)(2,1)}, u32[]{:S(2)}, u32[]{:S(2)}) collective-permute-start(bf16[128,2,3,16,128]{4,3,2,1,0:T(8,128)(2,1)} %all_to_all.10), channel_id=1, source_target_pairs={{0,1},{1,0},{2,3},{3,2},{4,5},{5,4},{6,7},{7,6},{8,9},{9,8},{10,11... | collective-permute-start | bytes 9437192 | tf_op jit(solution)/shard_map/ppermute | solution.py:199
  165.0 0.0 copy-done.3
  165.1 0.0 copy-done.4
  165.1 0.3 collective-permute-start.1
  165.4 6.4 %collective-permute-done.1 = bf16[256,2048]{1,0:T(8,128)(2,1)S(1)} collective-permute-done((bf16[256,2048]{1,0:T(8,128)(2,1)S(1)}, bf16[256,2048]{1,0:T(8,128)(2,1)S(1)}, u32[]{:S(2)}, u32[]{:S(2)}) %collective-permute-start.1) | collective-permute-done | bytes 1048608 | tf_op jit(solution)/shard_map/ppermute | solution.py:192
  171.8 1.0 maximum_select_fusion
  172.8 1.5 fusion
  174.3 0.0 copy-start
  174.3 13.7 %near.1 = (f32[256,4096]{1,0:T(8,128)}, f32[8,256,8]{2,1,0:T(8,128)}) custom-call(s32[1]{0:T(128)} %bitcast.5.core_ref, bf16[256,4096]{1,0:T(8,128)(2,1)} %q_ref.5, bf16[512,1024]{1,0:T(8,128)(2,1)} %get-tuple-element.10.k_ref, bf16[512,1024]{1,0:T(8,128)(2,1)} %get-tuple-element.9.v_ref), custom_call_target="tpu_custom_call" | custom-call | flops 2147483648 | bytes 9437184 | tf_op jit(solution)/shard_map/near/pallas_call | solution.py:97
  188.0 0.0 copy-done
  188.0 0.0 copy-start.1
  188.0 1.2 copy-done.1
  189.2 15.7 %far.2.rest_0_ = bf16[256,4096]{1,0:T(8,128)(2,1)} custom-call(s32[1]{0:T(128)} %bitcast.5.core_ref, bf16[256,4096]{1,0:T(8,128)(2,1)S(1)} %copy-done, bf16[32,4,2,3,16,128]{5,4,3,2,1,0:T(8,128)(2,1)} %bitcast.6.kv_ref, f32[256,4096]{1,0:T(8,128)} %get-tuple-element.7.acc_ref, f32[8,256,8]{2,1,0:T(8,128)S(1)} %copy-done.1), custom_call_target="tpu_custom_call" | custom-call | flops 3221225472 | bytes 7340032 | tf_op jit(solution)/shard_map/far/pallas_call | solution.py:163
  204.9 0.0 collective-permute-done
  204.9 15.7 %far.3 = bf16[256,4096]{1,0:T(8,128)(2,1)} custom-call(s32[1]{0:T(128)} %bitcast.core_ref, bf16[256,4096]{1,0:T(8,128)(2,1)S(1)} %copy-done, bf16[32,4,2,3,16,128]{5,4,3,2,1,0:T(8,128)(2,1)} %bitcast.4.kv_ref, f32[256,4096]{1,0:T(8,128)} %get-tuple-element.7.acc_ref, f32[8,256,8]{2,1,0:T(8,128)S(1)} %copy-done.1, ...), custom_call_target="tpu_custom_call", output_to_operand_aliasing={{}: (5, {})} | custom-call | flops 3221225472 | bytes 7340032 | tf_op jit(solution)/shard_map/far/pallas_call | solution.py:163
  (3 shorter events, 0.1 us)
Async XLA Ops:
  3.8 12.0 %copy-start.5 = (s32[4,1,3]{0,1,2:T(1,128)S(1)}, s32[4,1,3]{0,1,2:T(1,128)}, u32[]{:S(2)}) copy-start(s32[4,1,3]{0,1,2:T(1,128)} %param.11) | copy-start | bytes 148
  3.8 12.2 %copy-start.6 = (u32[256]{0:T(256)S(1)}, u32[256]{0:T(256)}, u32[]{:S(2)}) copy-start(u32[256]{0:T(256)} %constant.11) | copy-start | bytes 3076
  3.8 64.8 %all-to-all-start = ((bf16[32,2,8,16,128]{4,3,2,1,0:T(8,128)(2,1)}), bf16[32,2,8,16,128]{4,3,2,1,0:T(8,128)(2,1)S(1)}, u32[]{:S(2)}, u32[]{:S(2)}) async-start(bf16[32,2,8,16,128]{4,3,2,1,0:T(8,128)(2,1)} %spread.1), calls=%async_computation | async-start | bytes 4194304 | tf_op jit(solution)/shard_map/all_to_all | solution.py:187
  68.6 1.3 copy-start.2
  76.9 88.1 %copy-start.3 = (bf16[256,1024]{1,0:T(8,128)(2,1)S(1)}, bf16[256,1024]{1,0:T(8,128)(2,1)}, u32[]{:S(2)}) copy-start(bf16[256,1024]{1,0:T(8,128)(2,1)} %param.7) | copy-start | bytes 1572868
  76.9 88.2 %copy-start.4 = (bf16[256,1024]{1,0:T(8,128)(2,1)S(1)}, bf16[256,1024]{1,0:T(8,128)(2,1)}, u32[]{:S(2)}) copy-start(bf16[256,1024]{1,0:T(8,128)(2,1)} %param.8) | copy-start | bytes 1572868
  158.9 46.0 %collective-permute-start = (bf16[128,2,3,16,128]{4,3,2,1,0:T(8,128)(2,1)}, bf16[128,2,3,16,128]{4,3,2,1,0:T(8,128)(2,1)}, u32[]{:S(2)}, u32[]{:S(2)}) collective-permute-start(bf16[128,2,3,16,128]{4,3,2,1,0:T(8,128)(2,1)} %all_to_all.10), channel_id=1, source_target_pairs={{0,1},{1,0},{2,3},{3,2},{4,5},{5,4},{6,7},{7,6},{8,9},{9,8},{10,11... | collective-permute-start | bytes 9437192 | tf_op jit(solution)/shard_map/ppermute | solution.py:199
  165.1 6.7 %collective-permute-start.1 = (bf16[256,2048]{1,0:T(8,128)(2,1)S(1)}, bf16[256,2048]{1,0:T(8,128)(2,1)S(1)}, u32[]{:S(2)}, u32[]{:S(2)}) collective-permute-start(bf16[256,2048]{1,0:T(8,128)(2,1)S(1)} %constant_dynamic-update-slice_fusion), channel_id=1, source_target_pairs={{0,1},{1,0},{2,3},{3,2},{4,5},{5,4},{6,7},{7,6},{8,9},{9,8},{10,11... | collective-permute-start | bytes 3145736 | tf_op jit(solution)/shard_map/ppermute | solution.py:192
  174.3 13.7 %copy-start = (bf16[256,4096]{1,0:T(8,128)(2,1)S(1)}, bf16[256,4096]{1,0:T(8,128)(2,1)}, u32[]{:S(2)}) copy-start(bf16[256,4096]{1,0:T(8,128)(2,1)} %q_ref.5) | copy-start | bytes 6291460
  188.0 1.2 copy-start.1

commit v2 on v1

v2 whole, which is shorter than its diff:
```python
import functools
import math

import jax
import jax.numpy as jnp
from jax import lax
from jax.experimental import pallas as pl
from jax.experimental.pallas import tpu as pltpu
from jax.sharding import Mesh
from jax.sharding import PartitionSpec as P

HD = 128
BLK = 512
MIB = 1024 * 1024
EXP_SCALE = math.log2(math.e) / math.sqrt(HD)
NEG = -1e30
NT = (((1,), (1,)), ((), ()))
NN = (((1,), (0,)), ((), ()))


def in_hbm(x):
    return pltpu.with_memory_space_constraint(x, pltpu.HBM)


def spread_kernel(ids_ref, k_ref, v_ref, o_ref, cache, stage, sems, out_sems):
    blocks, pieces, rows, _ = k_ref.shape
    copies = []
    for b in range(blocks):
        copies.append(pltpu.make_async_copy(k_ref.at[b], cache.at[2 * b], sems.at[2 * b]))
        copies.append(pltpu.make_async_copy(v_ref.at[b], cache.at[2 * b + 1], sems.at[2 * b + 1]))
    for copy in copies:
        copy.start()
    lane = lax.broadcasted_iota(jnp.int32, (rows, HD), 1)
    ids = jnp.zeros((rows, HD), jnp.int32)
    picks, _, ys = ids_ref.shape
    for y in range(ys):
        for j in range(picks):
            ids = jnp.where(lane == y * picks + j, ids_ref[j, 0, y], ids)
    ids = ids.astype(jnp.float32).astype(stage.dtype)
    for m in range(pieces):
        stage[m, 2 * blocks] = ids
    for part in range(2 * blocks):
        copies[part].wait()
        if part < 2 * blocks - 1:
            for m in range(pieces):
                stage[m, part] = cache[part, m]
    outs = []
    step = pieces // out_sems.shape[0]
    for i in range(0, pieces, step):
        for m in range(i, i + step):
            stage[m, 2 * blocks - 1] = cache[2 * blocks - 1, m]
        outs.append(pltpu.make_async_copy(stage.at[i : i + step], o_ref.at[i : i + step], out_sems.at[i // step]))
        outs[-1].start()
    for copy in outs:
        copy.wait()


def spread(cache_keys, cache_values, chosen, pieces):
    blocks = cache_keys.shape[0] // BLK
    rows = BLK // pieces
    shape = (blocks, pieces, rows, HD)
    message = (pieces, 2 * blocks + 1, rows, HD)
    anywhere = pl.BlockSpec(memory_space=pl.ANY)
    return pl.pallas_call(
        spread_kernel,
        in_specs=[pl.BlockSpec(memory_space=pltpu.SMEM), anywhere, anywhere],
        out_specs=anywhere,
        out_shape=jax.ShapeDtypeStruct(message, cache_keys.dtype),
        scratch_shapes=[
            pltpu.VMEM((2 * blocks, pieces, rows, HD), cache_keys.dtype),
            pltpu.VMEM(message, cache_keys.dtype),
            pltpu.SemaphoreType.DMA((2 * blocks,)),
            pltpu.SemaphoreType.DMA((4,)),
        ],
        name="spread",
    )(chosen.transpose(2, 1, 0), *(in_hbm(x.reshape(shape)) for x in (cache_keys, cache_values)))


def pick_kernel(held_ref, o_ref, wide, ids, sem, *, step, ys, picks):
    sources, parts, _, _ = held_ref.shape
    blocks = (parts - 1) // 2
    at = pl.program_id(0)

    @pl.when(at == 0)
    def _():
        wide[...] = held_ref[:, 2 * blocks].astype(jnp.float32)[:, 0, :].astype(jnp.int32)
        copy = pltpu.make_async_copy(wide, ids, sem)
        copy.start()
        copy.wait()

    for i in range(step):
        for y in range(ys):
            for j in range(picks):
                block_id = ids[at * step + i, y * picks + j]
                src = lax.shift_right_logical(block_id, blocks.bit_length() - 1)
                part = 2 * (block_id & (blocks - 1))
                o_ref[i * ys + y, j] = held_ref[src, pl.ds(part, 2)]


def pick(held, ys, picks):
    sources, parts, rows, _ = held.shape
    step = 8
    return pl.pallas_call(
        functools.partial(pick_kernel, step=step, ys=ys, picks=picks),
        grid=(sources // step,),
        in_specs=[pl.BlockSpec(memory_space=pltpu.VMEM)],
        out_specs=pl.BlockSpec((step * ys, picks, 2, rows, HD), lambda i: (i, 0, 0, 0, 0)),
        out_shape=jax.ShapeDtypeStruct((sources * ys, picks, 2, rows, HD), held.dtype),
        scratch_shapes=[
            pltpu.VMEM((sources, HD), jnp.int32),
            pltpu.SMEM((sources, HD), jnp.int32),
            pltpu.SemaphoreType.DMA,
        ],
        compiler_params=pltpu.CompilerParams(vmem_limit_bytes=8 * MIB),
        name="pick",
    )(pltpu.with_memory_space_constraint(held, pltpu.VMEM))


def near_kernel(core_ref, q_ref, k_ref, v_ref, k2_ref, v2_ref, acc_ref, stat_ref, *, group):
    rows = q_ref.shape[0]
    row = lax.broadcasted_iota(jnp.int32, (rows, 2 * rows), 0)
    col = lax.broadcasted_iota(jnp.int32, (rows, 2 * rows), 1)
    seen = jnp.where(col < rows, col, jnp.where(core_ref[0] == 1, -1, 2 * rows)) <= row
    keys = jnp.concatenate([k_ref[...], k2_ref[...]])
    values = jnp.concatenate([v_ref[...], v2_ref[...]])
    for g in range(group):
        cols = slice(g * HD, (g + 1) * HD)
        raw = lax.dot_general(q_ref[:, cols], keys, NT, preferred_element_type=jnp.float32)
        raw = jnp.where(seen, raw, NEG)
        top = jnp.max(raw, axis=1, keepdims=True)
        weights = jnp.exp2((raw - top) * EXP_SCALE)
        total = jnp.sum(weights, axis=1, keepdims=True)
        acc_ref[:, cols] = lax.dot_general(
            weights.astype(jnp.bfloat16), values, NN, preferred_element_type=jnp.float32
        )
        stat_ref[0, :, 2 * g : 2 * g + 1] = top
        stat_ref[0, :, 2 * g + 1 : 2 * g + 2] = total


def near_part(core, queries, keys, values, their_keys, their_values):
    rows, width = queries.shape
    heads = keys.shape[1] // HD
    group = width // (heads * HD)
    head = pl.BlockSpec((rows, HD), lambda h, core: (0, h))
    return pl.pallas_call(
        functools.partial(near_kernel, group=group),
        grid_spec=pltpu.PrefetchScalarGridSpec(
            num_scalar_prefetch=1,
            grid=(heads,),
            in_specs=[pl.BlockSpec((rows, group * HD), lambda h, core: (0, h)), head, head, head, head],
            out_specs=[
                pl.BlockSpec((rows, group * HD), lambda h, core: (0, h)),
                pl.BlockSpec((1, rows, 2 * group), lambda h, core: (h, 0, 0)),
            ],
        ),
        out_shape=[
            jax.ShapeDtypeStruct((rows, width), jnp.float32),
            jax.ShapeDtypeStruct((heads, rows, 2 * group), jnp.float32),
        ],
        cost_estimate=pl.CostEstimate(
            flops=4 * rows * BLK * width, bytes_accessed=9 * rows * width, transcendentals=rows * BLK * width // HD
        ),
        name="near",
    )(core, queries, keys, values, their_keys, their_values)


def far_kernel(parity_ref, q_ref, kv_ref, acc_ref, stat_ref, *rest, group):
    o_ref = rest[-1]
    y = pl.program_id(0)
    pieces, _, picks, _, piece_rows, _ = kv_ref.shape
    far = pieces * picks * piece_rows
    at = y if kv_ref.shape[1] > 1 else 0
    keys = kv_ref[:, at, :, 0].reshape(far, HD)
    values = kv_ref[:, at, :, 1].reshape(far, HD)
    wide = jnp.concatenate([values, jnp.ones_like(values)], axis=1)
    stat = stat_ref[0]

    def columns(g):
        return slice(g * HD, (g + 1) * HD)

    def scores(g):
        return lax.dot_general(q_ref[:, columns(g)], keys, NT, preferred_element_type=jnp.float32)

    def weigh(g):
        return jnp.exp2(scores(g) * EXP_SCALE - stat[:, 2 * g : 2 * g + 1] * EXP_SCALE).astype(jnp.bfloat16)

    worst = jnp.zeros((q_ref.shape[0], 1), jnp.float32)
    ready = weigh(0)
    for g in range(group):
        weights = ready
        if g + 1 < group:
            ready = weigh(g + 1)
        mixed = lax.dot_general(weights, wide, NN, preferred_element_type=jnp.float32)
        total = mixed[:, HD : HD + 1] + stat[:, 2 * g + 1 : 2 * g + 2]
        worst = jnp.maximum(worst, total)
        o_ref[:, g * HD : (g + 1) * HD] = ((mixed[:, :HD] + acc_ref[:, columns(g)]) / total).astype(o_ref.dtype)

    @pl.when(jnp.logical_not(jnp.max(worst) < 2.0**100))
    def _():
        for g in range(group):
            near_top = stat[:, 2 * g : 2 * g + 1]
            raw = scores(g)
            top = jnp.maximum(jnp.max(raw, axis=1, keepdims=True), near_top)
            exact = jnp.exp2((raw - top) * EXP_SCALE)
            keep = jnp.exp2((near_top - top) * EXP_SCALE)
            total = jnp.sum(exact, axis=1, keepdims=True) + keep * stat[:, 2 * g + 1 : 2 * g + 2]
            mixed = lax.dot_general(exact.astype(jnp.bfloat16), values, NN, preferred_element_type=jnp.float32)
            mixed = (mixed + keep * acc_ref[:, columns(g)]) / total
            o_ref[:, g * HD : (g + 1) * HD] = mixed.astype(o_ref.dtype)


def far_part(parity, queries, kv, acc, stat, prior):
    rows, width = queries.shape
    pieces, ys, picks, _, piece_rows, _ = kv.shape
    heads = stat.shape[0]
    group = stat.shape[2] // 2
    per = heads // ys
    strip = pl.BlockSpec((rows, group * HD), lambda y, parity: (0, per * y + parity[0]))
    in_specs = [
        strip,
        pl.BlockSpec(memory_space=pltpu.VMEM),
        strip,
        pl.BlockSpec((1, rows, 2 * group), lambda y, parity: (per * y + parity[0], 0, 0)),
    ]
    queries, acc, stat = in_hbm(queries), in_hbm(acc), in_hbm(stat)
    aliases = {}
    if prior is None:
        operands = [parity, queries, pltpu.with_memory_space_constraint(kv, pltpu.VMEM), acc, stat]
    else:
        in_specs[1] = pl.BlockSpec((pieces, 1, picks, 2, piece_rows, HD), lambda y, parity: (0, y, 0, 0, 0, 0))
        in_specs.append(pl.BlockSpec(memory_space=pl.ANY))
        operands = [parity, queries, in_hbm(kv), acc, stat, prior]
        aliases = {5: 0}
    far = pieces * picks * piece_rows
    return pl.pallas_call(
        functools.partial(far_kernel, group=group),
        grid_spec=pltpu.PrefetchScalarGridSpec(
            num_scalar_prefetch=1,
            grid=(ys,),
            in_specs=in_specs,
            out_specs=strip,
        ),
        out_shape=jax.ShapeDtypeStruct((rows, width), queries.dtype),
        input_output_aliases=aliases,
        cost_estimate=pl.CostEstimate(
            flops=4 * rows * far * width // per,
            bytes_accessed=4 * rows * width + kv.size * 2,
            transcendentals=rows * far * width // HD // per,
        ),
        compiler_params=pltpu.CompilerParams(vmem_limit_bytes=32 * MIB),
        name="far",
    )(*operands)


def local(queries, new_keys, new_values, cache_keys, cache_values, chosen):
    ctx_size = lax.axis_size("ctx")
    ys = lax.axis_size("y")
    core = lax.axis_index("core").astype(jnp.int32)
    picks = chosen.shape[2]

    outgoing = spread(cache_keys, cache_values, chosen, ctx_size)
    held = lax.all_to_all(outgoing, "ctx", split_axis=0, concat_axis=0, tiled=True)

    swap = [(0, 1), (1, 0)]
    their_keys = lax.ppermute(new_keys, "core", swap)
    their_values = lax.ppermute(new_values, "core", swap)
    near = near_part(core.reshape(1), queries, new_keys, new_values, their_keys, their_values)
    held, (acc, stat) = lax.optimization_barrier((held, near))

    got = lax.all_to_all(pick(held, ys, picks), ("ctx", "y"), split_axis=0, concat_axis=0, tiled=True)
    other = lax.ppermute(got, "core", swap)
    split = (ctx_size, ys) + got.shape[1:]
    out = far_part(core.reshape(1), queries, got.reshape(split), acc, stat, None)
    other, out = lax.optimization_barrier((other, out))
    return far_part((1 - core).reshape(1), queries, other.reshape(split), acc, stat, out)


def solution(mesh):
    ctx_size, head_size = mesh.devices.shape
    fine = Mesh(mesh.devices.reshape(ctx_size, head_size // 2, 2), ("ctx", "y", "core"))
    rows = P(("ctx", "y", "core"), None)
    in_specs = (
        rows,
        rows,
        rows,
        P("ctx", ("y", "core")),
        P("ctx", ("y", "core")),
        P("ctx", ("y", "core"), None),
    )
    return jax.shard_map(local, mesh=fine, in_specs=in_specs, out_specs=rows, check_vma=False)
```

time: 221 us -> 176 us (0.80)
  blocking collectives: 133 us -> 81.1 us
  waiting for transfers between devices: 6.4 us -> 36.8 us
  Pallas kernels: 55.8 us -> 38.9 us
  local copies, waits for them, and re-layouts: 5.19 us -> 0.01 us
    unnamed x1 -> x0, blocking collectives: 51.1 us -> none
    all_to_all x1, waiting for transfers between devices: 0.01 us -> 34.5 us  [local(): lax.all_to_all(outgoing, 'ctx', split_axis=0, concat_axis=0, tiled=True)]
    pallas_call x2, Pallas kernels: 31.4 us -> 20.1 us  [far_part(): pl.pallas_call(functools.partial(far_kernel, group=group), grid_spec=pltp...]
    pallas_call x2, Pallas kernels: 10.7 us -> 5.65 us  [the longest x1 3.84 us: spread(): pl.pallas_call(spread_kernel, in_specs=[pl.BlockSpec(memory_space=pltpu.S...]
    ppermute x1 -> x2, waiting for transfers between devices: 6.4 us -> 2.31 us  [the longest x1 1.56 us: local(): their_keys = lax.ppermute(new_keys, 'core', swap)]
    unnamed x19 -> x4, local copies, waits for them, and re-layouts: 3.54 us -> 0.01 us
  transfers between devices with their start and end apart: 3 -> 4, of which waited for: 1 -> 3; matrix products, arithmetic and copies ran while one was open for 2% -> 0% of each run, Pallas kernels for 13% -> 13%
where the time goes in v2:
time: 176 us
  blocking collectives  81.1 us (46%)
  Pallas kernels  38.9 us (22%)
  waiting for transfers between devices  36.8 us (21%)
  starting transfers between devices  18.6 us (11%)
    all_to_all x1, blocking collectives, local(): lax.all_to_all(pick(held, ys, picks), ('ctx', 'y'), split_axis=0, concat_...  81.1 us
    all_to_all x1, waiting for transfers between devices, local(): lax.all_to_all(outgoing, 'ctx', split_axis=0, concat_axis=0, tiled=True)  34.5 us
    pallas_call x2, Pallas kernels, far_part(): pl.pallas_call(functools.partial(far_kernel, group=group), grid_spec=pltp...  20.1 us
    pallas_call x1, Pallas kernels, near_part(): pl.pallas_call(functools.partial(near_kernel, group=group), grid_spec=plt...  13.1 us
    all_to_all x1, starting transfers between devices, local(): lax.all_to_all(outgoing, 'ctx', split_axis=0, concat_axis=0, tiled=True)  12 us
    ppermute x1, starting transfers between devices, local(): other = lax.ppermute(got, 'core', swap)  5.48 us
    pallas_call x1, Pallas kernels, spread(): pl.pallas_call(spread_kernel, in_specs=[pl.BlockSpec(memory_space=pltpu.S...  3.84 us
  transfers between devices with their start and end apart: 4, of which 3 were waited for; matrix products, arithmetic and copies ran while one was open for 0% of the time, Pallas kernels for 13%

profile of v2, /device:TPU:1, one launch (start us, length us, event | category | flops | bytes accessed | tf_op | source)
XLA Modules:
  0.0 175.5 jit_solution(831187804165528707)
XLA Ops:
  0.0 3.8 %spread.1 = bf16[32,17,16,128]{3,2,1,0:T(8,128)(2,1)} custom-call(s32[3,1,4]{2,1,0:T(1,128)} %bitcast.10, bf16[8,32,16,128]{3,2,1,0:T(8,128)(2,1)} %bitcast.8, bf16[8,32,16,128]{3,2,1,0:T(8,128)(2,1)} %bitcast.9), custom_call_target="tpu_custom_call" | custom-call | tf_op jit(solution)/shard_map/spread/pallas_call | solution.py:64
  3.8 0.0 copy-start
  3.9 0.0 copy-start.1
  3.9 12.0 %all-to-all-start = ((bf16[32,17,16,128]{3,2,1,0:T(8,128)(2,1)}), bf16[32,17,16,128]{3,2,1,0:T(8,128)(2,1)S(1)}, u32[]{:S(2)}, u32[]{:S(2)}) async-start(bf16[32,17,16,128]{3,2,1,0:T(8,128)(2,1)} %spread.1), calls=%async_computation | async-start | bytes 4456448 | tf_op jit(solution)/shard_map/all_to_all | solution.py:262
  15.9 0.0 copy-done
  15.9 1.0 collective-permute-start
  16.9 0.0 copy-done.1
  16.9 0.1 collective-permute-start.1
  17.1 1.6 collective-permute-done.k2_ref
  18.6 0.7 collective-permute-done.1.v2_ref
  19.4 13.1 %near.1 = (f32[256,4096]{1,0:T(8,128)}, f32[8,256,8]{2,1,0:T(8,128)}) custom-call(s32[1]{0:T(128)} %bitcast.4.core_ref.parity_ref, bf16[256,4096]{1,0:T(8,128)(2,1)} %q_ref.5, bf16[256,1024]{1,0:T(8,128)(2,1)} %k_ref.1, bf16[256,1024]{1,0:T(8,128)(2,1)} %v_ref.1, bf16[256,1024]{1,0:T(8,128)(2,1)} %collective-permute-done.k2_ref, ...), custom_call_target="tpu_custom_call" | custom-call | flops 2147483648 | bytes 9437184 | tf_op jit(solution)/shard_map/near/pallas_call | solution.py:145
  32.5 34.5 %all-to-all-done.held_ref = bf16[32,17,16,128]{3,2,1,0:T(8,128)(2,1)S(1)} async-done(((bf16[32,17,16,128]{3,2,1,0:T(8,128)(2,1)}), bf16[32,17,16,128]{3,2,1,0:T(8,128)(2,1)S(1)}, u32[]{:S(2)}, u32[]{:S(2)}) %all-to-all-start) | async-done | bytes 2228256 | tf_op jit(solution)/shard_map/all_to_all | solution.py:262
  67.0 1.8 %pick.1 = bf16[128,3,2,16,128]{4,3,2,1,0:T(8,128)(2,1)S(1)} custom-call(bf16[32,17,16,128]{3,2,1,0:T(8,128)(2,1)S(1)} %all-to-all-done.held_ref), custom_call_target="tpu_custom_call" | custom-call | tf_op jit(solution)/shard_map/pick/pallas_call | solution.py:103
  68.8 81.1 %all_to_all.10 = bf16[128,3,2,16,128]{4,3,2,1,0:T(8,128)(2,1)S(1)} all-to-all(bf16[128,3,2,16,128]{4,3,2,1,0:T(8,128)(2,1)S(1)} %pick.1), channel_id=1, replica_groups=mesh['ctx'=32,'y'=4,'core'=2] {'ctx','y'}, dimensions={0} | all-to-all | bytes 6291456 | tf_op jit(solution)/shard_map/all_to_all | solution.py:270
  150.0 5.5 %collective-permute-start.2 = (bf16[128,3,2,16,128]{4,3,2,1,0:T(8,128)(2,1)S(1)}, bf16[128,3,2,16,128]{4,3,2,1,0:T(8,128)(2,1)}, u32[]{:S(2)}, u32[]{:S(2)}) collective-permute-start(bf16[128,3,2,16,128]{4,3,2,1,0:T(8,128)(2,1)S(1)} %all_to_all.10), channel_id=1, source_target_pairs={{0,1},{1,0},{2,3},{3,2},{4,5},{5,4},{6,7},{7,6},{8,9},{9,8},{10,11... | collective-permute-start | bytes 9437192 | tf_op jit(solution)/shard_map/ppermute | solution.py:271
  155.4 9.9 %far.2.rest_0_ = bf16[256,4096]{1,0:T(8,128)(2,1)} custom-call(s32[1]{0:T(128)} %bitcast.4.core_ref.parity_ref, bf16[256,4096]{1,0:T(8,128)(2,1)} %q_ref.5, bf16[32,4,3,2,16,128]{5,4,3,2,1,0:T(8,128)(2,1)S(1)} %bitcast.7, f32[256,4096]{1,0:T(8,128)} %get-tuple-element.15.acc_ref, f32[8,256,8]{2,1,0:T(8,128)} %get-tuple-element.16.stat_ref), custom_call_target="tpu_custom_call" | custom-call | flops 3221225472 | bytes 7340032 | tf_op jit(solution)/shard_map/far/pallas_call | solution.py:235
  165.4 0.0 collective-permute-done.2
  165.4 10.2 %far.3 = bf16[256,4096]{1,0:T(8,128)(2,1)} custom-call(s32[1]{0:T(128)} %bitcast.parity_ref, bf16[256,4096]{1,0:T(8,128)(2,1)} %q_ref.5, bf16[32,4,3,2,16,128]{5,4,3,2,1,0:T(8,128)(2,1)} %bitcast.6.kv_ref, f32[256,4096]{1,0:T(8,128)} %get-tuple-element.15.acc_ref, f32[8,256,8]{2,1,0:T(8,128)} %get-tuple-element.16.stat_ref, ...), custom_call_target="tpu_custom_call", output_to_operand_aliasing={{}: (5, {})} | custom-call | flops 3221225472 | bytes 7340032 | tf_op jit(solution)/shard_map/far/pallas_call | solution.py:235
Async XLA Ops:
  3.8 12.0 %copy-start = (bf16[256,1024]{1,0:T(8,128)(2,1)S(1)}, bf16[256,1024]{1,0:T(8,128)(2,1)}, u32[]{:S(2)}) copy-start(bf16[256,1024]{1,0:T(8,128)(2,1)} %k_ref.1) | copy-start | bytes 1572868
  3.9 13.1 %copy-start.1 = (bf16[256,1024]{1,0:T(8,128)(2,1)S(1)}, bf16[256,1024]{1,0:T(8,128)(2,1)}, u32[]{:S(2)}) copy-start(bf16[256,1024]{1,0:T(8,128)(2,1)} %v_ref.1) | copy-start | bytes 1572868
  3.9 63.1 %all-to-all-start = ((bf16[32,17,16,128]{3,2,1,0:T(8,128)(2,1)}), bf16[32,17,16,128]{3,2,1,0:T(8,128)(2,1)S(1)}, u32[]{:S(2)}, u32[]{:S(2)}) async-start(bf16[32,17,16,128]{3,2,1,0:T(8,128)(2,1)} %spread.1), calls=%async_computation | async-start | bytes 4456448 | tf_op jit(solution)/shard_map/all_to_all | solution.py:262
  15.9 2.7 %collective-permute-start = (bf16[256,1024]{1,0:T(8,128)(2,1)S(1)}, bf16[256,1024]{1,0:T(8,128)(2,1)}, u32[]{:S(2)}, u32[]{:S(2)}) collective-permute-start(bf16[256,1024]{1,0:T(8,128)(2,1)S(1)} %copy-done), channel_id=1, source_target_pairs={{0,1},{1,0},{2,3},{3,2},{4,5},{5,4},{6,7},{7,6},{8,9},{9,8},{10,11... | collective-permute-start | bytes 1572872 | tf_op jit(solution)/shard_map/ppermute | solution.py:265
  16.9 2.4 %collective-permute-start.1 = (bf16[256,1024]{1,0:T(8,128)(2,1)S(1)}, bf16[256,1024]{1,0:T(8,128)(2,1)}, u32[]{:S(2)}, u32[]{:S(2)}) collective-permute-start(bf16[256,1024]{1,0:T(8,128)(2,1)S(1)} %copy-done.1), channel_id=1, source_target_pairs={{0,1},{1,0},{2,3},{3,2},{4,5},{5,4},{6,7},{7,6},{8,9},{9,8},{10,11... | collective-permute-start | bytes 1572872 | tf_op jit(solution)/shard_map/ppermute | solution.py:266
  150.0 15.4 %collective-permute-start.2 = (bf16[128,3,2,16,128]{4,3,2,1,0:T(8,128)(2,1)S(1)}, bf16[128,3,2,16,128]{4,3,2,1,0:T(8,128)(2,1)}, u32[]{:S(2)}, u32[]{:S(2)}) collective-permute-start(bf16[128,3,2,16,128]{4,3,2,1,0:T(8,128)(2,1)S(1)} %all_to_all.10), channel_id=1, source_target_pairs={{0,1},{1,0},{2,3},{3,2},{4,5},{5,4},{6,7},{7,6},{8,9},{9,8},{10,11... | collective-permute-start | bytes 9437192 | tf_op jit(solution)/shard_map/ppermute | solution.py:271

commit v3 on v2

v3 whole, which is shorter than its diff:
```python
import functools
import math

import jax
import jax.numpy as jnp
from jax import lax
from jax.experimental import pallas as pl
from jax.experimental.pallas import tpu as pltpu
from jax.sharding import Mesh
from jax.sharding import PartitionSpec as P

HD = 128
BLK = 512
MIB = 1024 * 1024
EXP_SCALE = math.log2(math.e) / math.sqrt(HD)
NEG = -1e30
NT = (((1,), (1,)), ((), ()))
NN = (((1,), (0,)), ((), ()))


def in_hbm(x):
    return pltpu.with_memory_space_constraint(x, pltpu.HBM)


def spread_kernel(chosen_ref, k_ref, v_ref, o_ref, chosen, cache, stage, sems, out_sems, fetch_sem):
    blocks, pieces, rows, _ = k_ref.shape
    groups = out_sems.shape[0]
    parts = [pl.ds(i * (pieces // groups), pieces // groups) for i in range(groups)]
    copies = [
        [pltpu.make_async_copy(ref.at[:, part], cache.at[at, :, part], sems.at[at, i]) for at, ref in enumerate((k_ref, v_ref))]
        for i, part in enumerate(parts)
    ]
    fetch = pltpu.make_async_copy(chosen_ref, chosen, fetch_sem)
    fetch.start()
    for pair in copies:
        for copy in pair:
            copy.start()
    fetch.wait()
    lane = lax.broadcasted_iota(jnp.int32, (rows, HD), 1)
    ids = jnp.zeros((rows, HD), jnp.int32)
    picks, _, ys = chosen.shape
    for y in range(ys):
        for j in range(picks):
            ids = jnp.where(lane == y * picks + j, chosen[j, 0, y], ids)
    ids = ids.astype(jnp.float32).astype(stage.dtype)
    outs = []
    for i, part in enumerate(parts):
        for copy in copies[i]:
            copy.wait()
        for m in range(part.start, part.start + part.size):
            for b in range(blocks):
                stage[m, 2 * b] = cache[0, b, m]
                stage[m, 2 * b + 1] = cache[1, b, m]
            stage[m, 2 * blocks] = ids
        outs.append(pltpu.make_async_copy(stage.at[part], o_ref.at[part], out_sems.at[i]))
        outs[-1].start()
    for copy in outs:
        copy.wait()


def spread(cache_keys, cache_values, chosen, pieces):
    blocks = cache_keys.shape[0] // BLK
    rows = BLK // pieces
    shape = (blocks, pieces, rows, HD)
    message = (pieces, 2 * blocks + 1, rows, HD)
    anywhere = pl.BlockSpec(memory_space=pl.ANY)
    groups = 4
    return pl.pallas_call(
        spread_kernel,
        in_specs=[anywhere, anywhere, anywhere],
        out_specs=anywhere,
        out_shape=pltpu.HBM(message, cache_keys.dtype),
        scratch_shapes=[
            pltpu.SMEM(chosen.shape[::-1], chosen.dtype),
            pltpu.VMEM((2,) + shape, cache_keys.dtype),
            pltpu.VMEM(message, cache_keys.dtype),
            pltpu.SemaphoreType.DMA((2, groups)),
            pltpu.SemaphoreType.DMA((groups,)),
            pltpu.SemaphoreType.DMA,
        ],
        compiler_params=pltpu.CompilerParams(vmem_limit_bytes=8 * MIB),
        name="spread",
    )(*(in_hbm(x) for x in (chosen.transpose(2, 1, 0), cache_keys.reshape(shape), cache_values.reshape(shape))))


def pick_kernel(held_ref, o_ref, wide, ids, sem, *, step, ys, picks):
    sources, parts, _, _ = held_ref.shape
    blocks = (parts - 1) // 2
    at = pl.program_id(0)

    @pl.when(at == 0)
    def _():
        wide[...] = held_ref[:, 2 * blocks].astype(jnp.float32)[:, 0, :].astype(jnp.int32)
        copy = pltpu.make_async_copy(wide, ids, sem)
        copy.start()
        copy.wait()

    for i in range(step):
        for y in range(ys):
            for j in range(picks):
                block_id = ids[at * step + i, y * picks + j]
                src = lax.shift_right_logical(block_id, blocks.bit_length() - 1)
                part = 2 * (block_id & (blocks - 1))
                o_ref[i * ys + y, j] = held_ref[src, pl.ds(part, 2)]


def pick(held, ys, picks):
    sources, parts, rows, _ = held.shape
    step = 8
    return pl.pallas_call(
        functools.partial(pick_kernel, step=step, ys=ys, picks=picks),
        grid=(sources // step,),
        in_specs=[pl.BlockSpec(memory_space=pltpu.VMEM)],
        out_specs=pl.BlockSpec((step * ys, picks, 2, rows, HD), lambda i: (i, 0, 0, 0, 0)),
        out_shape=jax.ShapeDtypeStruct((sources * ys, picks, 2, rows, HD), held.dtype),
        scratch_shapes=[
            pltpu.VMEM((sources, HD), jnp.int32),
            pltpu.SMEM((sources, HD), jnp.int32),
            pltpu.SemaphoreType.DMA,
        ],
        compiler_params=pltpu.CompilerParams(vmem_limit_bytes=8 * MIB),
        name="pick",
    )(pltpu.with_memory_space_constraint(held, pltpu.VMEM))


def near_kernel(core_ref, q_ref, k_ref, v_ref, k2_ref, v2_ref, acc_ref, stat_ref, *, group):
    rows = q_ref.shape[0]
    key = lax.broadcasted_iota(jnp.int32, (2 * rows, rows), 0)
    query = lax.broadcasted_iota(jnp.int32, (2 * rows, rows), 1)
    seen = jnp.where(key < rows, key, jnp.where(core_ref[0] == 1, -1, 2 * rows)) <= query
    keys = jnp.concatenate([k_ref[...], k2_ref[...]])
    values = jnp.concatenate([v_ref[...], v2_ref[...]]).T
    for g in range(group):
        cols = slice(g * HD, (g + 1) * HD)
        raw = lax.dot_general(keys, q_ref[:, cols], NT, preferred_element_type=jnp.float32)
        raw = jnp.where(seen, raw, NEG)
        top = jnp.max(raw, axis=0, keepdims=True)
        weights = jnp.exp2((raw - top) * EXP_SCALE)
        stat_ref[0, 2 * g : 2 * g + 1] = top
        stat_ref[0, 2 * g + 1 : 2 * g + 2] = jnp.sum(weights, axis=0, keepdims=True)
        acc_ref[0, cols] = lax.dot_general(
            values, weights.astype(jnp.bfloat16), NN, preferred_element_type=jnp.float32
        )


def near_part(core, queries, keys, values, their_keys, their_values):
    rows, width = queries.shape
    heads = keys.shape[1] // HD
    strip = width // heads
    group = strip // HD
    head = pl.BlockSpec((rows, HD), lambda h, core: (0, h))
    return pl.pallas_call(
        functools.partial(near_kernel, group=group),
        grid_spec=pltpu.PrefetchScalarGridSpec(
            num_scalar_prefetch=1,
            grid=(heads,),
            in_specs=[pl.BlockSpec((rows, strip), lambda h, core: (0, h)), head, head, head, head],
            out_specs=[
                pl.BlockSpec((1, strip, rows), lambda h, core: (h, 0, 0)),
                pl.BlockSpec((1, 2 * group, rows), lambda h, core: (h, 0, 0)),
            ],
        ),
        out_shape=[
            pltpu.HBM((heads, strip, rows), jnp.float32),
            pltpu.HBM((heads, 2 * group, rows), jnp.float32),
        ],
        cost_estimate=pl.CostEstimate(
            flops=4 * rows * BLK * width, bytes_accessed=9 * rows * width, transcendentals=rows * BLK * width // HD
        ),
        compiler_params=pltpu.CompilerParams(vmem_limit_bytes=24 * MIB),
        name="near",
    )(core, *(in_hbm(x) for x in (queries, keys, values, their_keys, their_values)))


def far_kernel(parity_ref, q_ref, kv_ref, acc_ref, stat_ref, *rest, group):
    o_ref = rest[-1]
    pieces, _, picks, _, piece_rows, _ = kv_ref.shape
    far = pieces * picks * piece_rows
    at = pl.program_id(0) if kv_ref.shape[1] > 1 else 0
    keys = kv_ref[:, at, :, 0].reshape(far, HD)
    values = kv_ref[:, at, :, 1].reshape(far, HD).T
    tall = jnp.concatenate([values, jnp.ones((16, far), values.dtype)], axis=0)

    def columns(g):
        return slice(g * HD, (g + 1) * HD)

    def near_top(g):
        return stat_ref[0, 2 * g : 2 * g + 1]

    def scores(g):
        return lax.dot_general(keys, q_ref[:, columns(g)], NT, preferred_element_type=jnp.float32)

    def weigh(g):
        return jnp.exp2(scores(g) * EXP_SCALE - near_top(g) * EXP_SCALE).astype(jnp.bfloat16)

    def put(g, weights, keep):
        mixed = lax.dot_general(tall, weights, NN, preferred_element_type=jnp.float32)
        total = mixed[HD : HD + 1] + keep * stat_ref[0, 2 * g + 1 : 2 * g + 2]
        mixed = (mixed[:HD] + keep * acc_ref[0, columns(g)]) / total
        o_ref[:, columns(g)] = mixed.T.astype(o_ref.dtype)
        return total

    worst = 0.0
    ready = weigh(0)
    for g in range(group):
        weights = ready
        if g + 1 < group:
            ready = weigh(g + 1)
        worst = jnp.maximum(worst, put(g, weights, 1.0))

    @pl.when(jnp.logical_not(jnp.max(worst) < 2.0**100))
    def _():
        for g in range(group):
            raw = scores(g)
            top = jnp.maximum(jnp.max(raw, axis=0, keepdims=True), near_top(g))
            exact = jnp.exp2((raw - top) * EXP_SCALE).astype(jnp.bfloat16)
            put(g, exact, jnp.exp2((near_top(g) - top) * EXP_SCALE))


def far_part(parity, queries, kv, acc, stat, prior):
    rows, width = queries.shape
    pieces, ys, picks, _, piece_rows, _ = kv.shape
    heads, strip, _ = acc.shape
    per = heads // ys
    columns = pl.BlockSpec((rows, strip), lambda y, parity: (0, per * y + parity[0]))
    in_specs = [
        columns,
        pl.BlockSpec(memory_space=pltpu.VMEM),
        pl.BlockSpec((1, strip, rows), lambda y, parity: (per * y + parity[0], 0, 0)),
        pl.BlockSpec((1, stat.shape[1], rows), lambda y, parity: (per * y + parity[0], 0, 0)),
    ]
    operands = [parity, in_hbm(queries), pltpu.with_memory_space_constraint(kv, pltpu.VMEM), in_hbm(acc), in_hbm(stat)]
    aliases = {}
    if prior is not None:
        in_specs[1] = pl.BlockSpec((pieces, 1, picks, 2, piece_rows, HD), lambda y, parity: (0, y, 0, 0, 0, 0))
        in_specs.append(pl.BlockSpec(memory_space=pl.ANY))
        operands[2] = in_hbm(kv)
        operands.append(prior)
        aliases = {5: 0}
    far = pieces * picks * piece_rows
    return pl.pallas_call(
        functools.partial(far_kernel, group=strip // HD),
        grid_spec=pltpu.PrefetchScalarGridSpec(
            num_scalar_prefetch=1, grid=(ys,), in_specs=in_specs, out_specs=columns
        ),
        out_shape=jax.ShapeDtypeStruct((rows, width), queries.dtype),
        input_output_aliases=aliases,
        cost_estimate=pl.CostEstimate(
            flops=4 * rows * far * width // per,
            bytes_accessed=4 * rows * width + kv.size * 2,
            transcendentals=rows * far * width // HD // per,
        ),
        compiler_params=pltpu.CompilerParams(vmem_limit_bytes=32 * MIB),
        name="far",
    )(*operands)


def local(queries, new_keys, new_values, cache_keys, cache_values, chosen):
    ctx_size = lax.axis_size("ctx")
    ys = lax.axis_size("y")
    core = lax.axis_index("core").astype(jnp.int32)
    picks = chosen.shape[2]

    outgoing = spread(cache_keys, cache_values, chosen, ctx_size)
    held = lax.all_to_all(outgoing, "ctx", split_axis=0, concat_axis=0, tiled=True)

    swap = [(0, 1), (1, 0)]
    their_keys = lax.ppermute(new_keys, "core", swap)
    their_values = lax.ppermute(new_values, "core", swap)
    near = near_part(core.reshape(1), queries, new_keys, new_values, their_keys, their_values)
    held, (acc, stat) = lax.optimization_barrier((held, near))

    got = lax.all_to_all(pick(held, ys, picks), ("ctx", "y"), split_axis=0, concat_axis=0, tiled=True)
    other = lax.ppermute(got, "core", swap)
    split = (ctx_size, ys) + got.shape[1:]
    out = far_part(core.reshape(1), queries, got.reshape(split), acc, stat, None)
    other, out = lax.optimization_barrier((other, out))
    return far_part((1 - core).reshape(1), queries, other.reshape(split), acc, stat, out)


def solution(mesh):
    ctx_size, head_size = mesh.devices.shape
    fine = Mesh(mesh.devices.reshape(ctx_size, head_size // 2, 2), ("ctx", "y", "core"))
    rows = P(("ctx", "y", "core"), None)
    in_specs = (
        rows,
        rows,
        rows,
        P("ctx", ("y", "core")),
        P("ctx", ("y", "core")),
        P("ctx", ("y", "core"), None),
    )
    return jax.shard_map(local, mesh=fine, in_specs=in_specs, out_specs=rows, check_vma=False)
```

time: 176 us -> 173 us (0.983)
  waiting for transfers between devices: 36.8 us -> 34 us
    all_to_all x1, waiting for transfers between devices: 34.5 us -> 31.7 us  [local(): lax.all_to_all(outgoing, 'ctx', split_axis=0, concat_axis=0, tiled=True)]
    pallas_call x1, Pallas kernels: 13.1 us -> 16 us  [near_part(): pl.pallas_call(functools.partial(near_kernel, group=group), grid_spec=plt...]
    pallas_call x3, Pallas kernels: 23.9 us -> 21.1 us  [the longest x2 18.6 us: far_part(): pl.pallas_call(functools.partial(far_kernel, group=strip // HD), grid_spe...]
  transfers between devices with their start and end apart: 4 -> 4, of which waited for: 3 -> 3; matrix products, arithmetic and copies ran while one was open for 0% -> 0% of each run, Pallas kernels for 13% -> 15%
where the time goes in v3:
time: 173 us
  blocking collectives  81.1 us (47%)
  Pallas kernels  38.9 us (22%)
  waiting for transfers between devices  34 us (20%)
  starting transfers between devices  18.6 us (11%)
    all_to_all x1, blocking collectives, local(): lax.all_to_all(pick(held, ys, picks), ('ctx', 'y'), split_axis=0, concat_...  81.1 us
    all_to_all x1, waiting for transfers between devices, local(): lax.all_to_all(outgoing, 'ctx', split_axis=0, concat_axis=0, tiled=True)  31.7 us
    pallas_call x2, Pallas kernels, far_part(): pl.pallas_call(functools.partial(far_kernel, group=strip // HD), grid_spe...  18.6 us
    pallas_call x1, Pallas kernels, near_part(): pl.pallas_call(functools.partial(near_kernel, group=group), grid_spec=plt...  16 us
    all_to_all x1, starting transfers between devices, local(): lax.all_to_all(outgoing, 'ctx', split_axis=0, concat_axis=0, tiled=True)  12 us
    ppermute x1, starting transfers between devices, local(): other = lax.ppermute(got, 'core', swap)  5.48 us
  transfers between devices with their start and end apart: 4, of which 3 were waited for; matrix products, arithmetic and copies ran while one was open for 0% of the time, Pallas kernels for 15%

profile of v3, /device:TPU:1, one launch (start us, length us, event | category | flops | bytes accessed | tf_op | source)
XLA Modules:
  0.0 172.8 jit_solution(5931082675010476599)
XLA Ops:
  0.0 2.6 %spread.1 = bf16[32,17,16,128]{3,2,1,0:T(8,128)(2,1)} custom-call(s32[3,1,4]{2,1,0:T(1,128)} %bitcast.10, bf16[8,32,16,128]{3,2,1,0:T(8,128)(2,1)} %bitcast.8, bf16[8,32,16,128]{3,2,1,0:T(8,128)(2,1)} %bitcast.9), custom_call_target="tpu_custom_call" | custom-call | tf_op jit(solution)/shard_map/spread/pallas_call | solution.py:68
  2.6 0.0 copy-start
  2.6 0.0 copy-start.1
  2.6 12.0 %all-to-all-start = ((bf16[32,17,16,128]{3,2,1,0:T(8,128)(2,1)}), bf16[32,17,16,128]{3,2,1,0:T(8,128)(2,1)S(1)}, u32[]{:S(2)}, u32[]{:S(2)}) async-start(bf16[32,17,16,128]{3,2,1,0:T(8,128)(2,1)} %spread.1), calls=%async_computation | async-start | bytes 4456448 | tf_op jit(solution)/shard_map/all_to_all | solution.py:265
  14.6 0.0 copy-done
  14.6 1.0 collective-permute-start
  15.7 0.0 copy-done.1
  15.7 0.1 collective-permute-start.1
  15.8 1.6 collective-permute-done.k2_ref
  17.3 0.7 collective-permute-done.1.v2_ref
  18.1 16.0 %near.1 = (f32[8,512,256]{2,1,0:T(8,128)}, f32[8,8,256]{2,1,0:T(8,128)}) custom-call(s32[1]{0:T(128)} %bitcast.4.core_ref.parity_ref, bf16[256,4096]{1,0:T(8,128)(2,1)} %q_ref.5, bf16[256,1024]{1,0:T(8,128)(2,1)} %k_ref.1, bf16[256,1024]{1,0:T(8,128)(2,1)} %v_ref.1, bf16[256,1024]{1,0:T(8,128)(2,1)} %collective-permute-done.k2_ref, ...), custom_call_target="tpu_custom_call" | custom-call | flops 2147483648 | bytes 9437184 | tf_op jit(solution)/shard_map/near/pallas_call | solution.py:152
  34.1 31.7 %all-to-all-done.held_ref = bf16[32,17,16,128]{3,2,1,0:T(8,128)(2,1)S(1)} async-done(((bf16[32,17,16,128]{3,2,1,0:T(8,128)(2,1)}), bf16[32,17,16,128]{3,2,1,0:T(8,128)(2,1)S(1)}, u32[]{:S(2)}, u32[]{:S(2)}) %all-to-all-start) | async-done | bytes 2228256 | tf_op jit(solution)/shard_map/all_to_all | solution.py:265
  65.7 1.8 %pick.1 = bf16[128,3,2,16,128]{4,3,2,1,0:T(8,128)(2,1)S(1)} custom-call(bf16[32,17,16,128]{3,2,1,0:T(8,128)(2,1)S(1)} %all-to-all-done.held_ref), custom_call_target="tpu_custom_call" | custom-call | tf_op jit(solution)/shard_map/pick/pallas_call | solution.py:110
  67.6 81.1 %all_to_all.10 = bf16[128,3,2,16,128]{4,3,2,1,0:T(8,128)(2,1)S(1)} all-to-all(bf16[128,3,2,16,128]{4,3,2,1,0:T(8,128)(2,1)S(1)} %pick.1), channel_id=1, replica_groups=mesh['ctx'=32,'y'=4,'core'=2] {'ctx','y'}, dimensions={0} | all-to-all | bytes 6291456 | tf_op jit(solution)/shard_map/all_to_all | solution.py:273
  148.7 5.5 %collective-permute-start.2 = (bf16[128,3,2,16,128]{4,3,2,1,0:T(8,128)(2,1)S(1)}, bf16[128,3,2,16,128]{4,3,2,1,0:T(8,128)(2,1)}, u32[]{:S(2)}, u32[]{:S(2)}) collective-permute-start(bf16[128,3,2,16,128]{4,3,2,1,0:T(8,128)(2,1)S(1)} %all_to_all.10), channel_id=1, source_target_pairs={{0,1},{1,0},{2,3},{3,2},{4,5},{5,4},{6,7},{7,6},{8,9},{9,8},{10,11... | collective-permute-start | bytes 9437192 | tf_op jit(solution)/shard_map/ppermute | solution.py:274
  154.2 9.1 %far.2.rest_0_ = bf16[256,4096]{1,0:T(8,128)(2,1)} custom-call(s32[1]{0:T(128)} %bitcast.4.core_ref.parity_ref, bf16[256,4096]{1,0:T(8,128)(2,1)} %q_ref.5, bf16[32,4,3,2,16,128]{5,4,3,2,1,0:T(8,128)(2,1)S(1)} %bitcast.7, f32[8,512,256]{2,1,0:T(8,128)} %get-tuple-element.15.acc_ref, f32[8,8,256]{2,1,0:T(8,128)} %get-tuple-element.16.stat_ref), custom_call_target="tpu_custom_call" | custom-call | flops 3221225472 | bytes 7340032 | tf_op jit(solution)/shard_map/far/pallas_call | solution.py:241
  163.3 0.0 collective-permute-done.2
  163.3 9.4 %far.3 = bf16[256,4096]{1,0:T(8,128)(2,1)} custom-call(s32[1]{0:T(128)} %bitcast.parity_ref, bf16[256,4096]{1,0:T(8,128)(2,1)} %q_ref.5, bf16[32,4,3,2,16,128]{5,4,3,2,1,0:T(8,128)(2,1)} %bitcast.6.kv_ref, f32[8,512,256]{2,1,0:T(8,128)} %get-tuple-element.15.acc_ref, f32[8,8,256]{2,1,0:T(8,128)} %get-tuple-element.16.stat_ref, ...), custom_call_target="tpu_custom_call", output_to_operand_aliasing={{}: (5, {})} | custom-call | flops 3221225472 | bytes 7340032 | tf_op jit(solution)/shard_map/far/pallas_call | solution.py:241
Async XLA Ops:
  2.6 12.0 %copy-start = (bf16[256,1024]{1,0:T(8,128)(2,1)S(1)}, bf16[256,1024]{1,0:T(8,128)(2,1)}, u32[]{:S(2)}) copy-start(bf16[256,1024]{1,0:T(8,128)(2,1)} %k_ref.1) | copy-start | bytes 1572868
  2.6 13.1 %copy-start.1 = (bf16[256,1024]{1,0:T(8,128)(2,1)S(1)}, bf16[256,1024]{1,0:T(8,128)(2,1)}, u32[]{:S(2)}) copy-start(bf16[256,1024]{1,0:T(8,128)(2,1)} %v_ref.1) | copy-start | bytes 1572868
  2.6 63.1 %all-to-all-start = ((bf16[32,17,16,128]{3,2,1,0:T(8,128)(2,1)}), bf16[32,17,16,128]{3,2,1,0:T(8,128)(2,1)S(1)}, u32[]{:S(2)}, u32[]{:S(2)}) async-start(bf16[32,17,16,128]{3,2,1,0:T(8,128)(2,1)} %spread.1), calls=%async_computation | async-start | bytes 4456448 | tf_op jit(solution)/shard_map/all_to_all | solution.py:265
  14.6 2.7 %collective-permute-start = (bf16[256,1024]{1,0:T(8,128)(2,1)S(1)}, bf16[256,1024]{1,0:T(8,128)(2,1)}, u32[]{:S(2)}, u32[]{:S(2)}) collective-permute-start(bf16[256,1024]{1,0:T(8,128)(2,1)S(1)} %copy-done), channel_id=1, source_target_pairs={{0,1},{1,0},{2,3},{3,2},{4,5},{5,4},{6,7},{7,6},{8,9},{9,8},{10,11... | collective-permute-start | bytes 1572872 | tf_op jit(solution)/shard_map/ppermute | solution.py:268
  15.7 2.4 %collective-permute-start.1 = (bf16[256,1024]{1,0:T(8,128)(2,1)S(1)}, bf16[256,1024]{1,0:T(8,128)(2,1)}, u32[]{:S(2)}, u32[]{:S(2)}) collective-permute-start(bf16[256,1024]{1,0:T(8,128)(2,1)S(1)} %copy-done.1), channel_id=1, source_target_pairs={{0,1},{1,0},{2,3},{3,2},{4,5},{5,4},{6,7},{7,6},{8,9},{9,8},{10,11... | collective-permute-start | bytes 1572872 | tf_op jit(solution)/shard_map/ppermute | solution.py:269
  148.7 14.6 %collective-permute-start.2 = (bf16[128,3,2,16,128]{4,3,2,1,0:T(8,128)(2,1)S(1)}, bf16[128,3,2,16,128]{4,3,2,1,0:T(8,128)(2,1)}, u32[]{:S(2)}, u32[]{:S(2)}) collective-permute-start(bf16[128,3,2,16,128]{4,3,2,1,0:T(8,128)(2,1)S(1)} %all_to_all.10), channel_id=1, source_target_pairs={{0,1},{1,0},{2,3},{3,2},{4,5},{5,4},{6,7},{7,6},{8,9},{9,8},{10,11... | collective-permute-start | bytes 9437192 | tf_op jit(solution)/shard_map/ppermute | solution.py:274

commit v4 on v3

--- a/solution.py
+++ b/solution.py
@@ -14,6 +14,7 @@
 MIB = 1024 * 1024
 EXP_SCALE = math.log2(math.e) / math.sqrt(HD)
 NEG = -1e30
+ID_ROWS = 8
 NT = (((1,), (1,)), ((), ()))
 NN = (((1,), (0,)), ((), ()))
 
@@ -36,8 +37,8 @@
         for copy in pair:
             copy.start()
     fetch.wait()
-    lane = lax.broadcasted_iota(jnp.int32, (rows, HD), 1)
-    ids = jnp.zeros((rows, HD), jnp.int32)
+    lane = lax.broadcasted_iota(jnp.int32, (ID_ROWS, HD), 1)
+    ids = jnp.zeros((ID_ROWS, HD), jnp.int32)
     picks, _, ys = chosen.shape
     for y in range(ys):
         for j in range(picks):
@@ -49,9 +50,9 @@
             copy.wait()
         for m in range(part.start, part.start + part.size):
             for b in range(blocks):
-                stage[m, 2 * b] = cache[0, b, m]
-                stage[m, 2 * b + 1] = cache[1, b, m]
-            stage[m, 2 * blocks] = ids
+                for at in range(2):
+                    stage[m, pl.ds((2 * b + at) * rows, rows)] = cache[at, b, m]
+            stage[m, pl.ds(2 * blocks * rows, ID_ROWS)] = ids
         outs.append(pltpu.make_async_copy(stage.at[part], o_ref.at[part], out_sems.at[i]))
         outs[-1].start()
     for copy in outs:
@@ -62,7 +63,7 @@
     blocks = cache_keys.shape[0] // BLK
     rows = BLK // pieces
     shape = (blocks, pieces, rows, HD)
-    message = (pieces, 2 * blocks + 1, rows, HD)
+    message = (pieces, 2 * blocks * rows + ID_ROWS, HD)
     anywhere = pl.BlockSpec(memory_space=pl.ANY)
     groups = 4
     return pl.pallas_call(
@@ -83,14 +84,13 @@
     )(*(in_hbm(x) for x in (chosen.transpose(2, 1, 0), cache_keys.reshape(shape), cache_values.reshape(shape))))
 
 
-def pick_kernel(held_ref, o_ref, wide, ids, sem, *, step, ys, picks):
-    sources, parts, _, _ = held_ref.shape
-    blocks = (parts - 1) // 2
+def pick_kernel(held_ref, o_ref, wide, ids, sem, *, step, ys, picks, blocks, rows):
     at = pl.program_id(0)
 
     @pl.when(at == 0)
     def _():
-        wide[...] = held_ref[:, 2 * blocks].astype(jnp.float32)[:, 0, :].astype(jnp.int32)
+        tail = held_ref[:, 2 * blocks * rows :].astype(jnp.float32)
+        wide[...] = tail[:, 0, :].astype(jnp.int32)
         copy = pltpu.make_async_copy(wide, ids, sem)
         copy.start()
         copy.wait()
@@ -100,15 +100,16 @@
             for j in range(picks):
                 block_id = ids[at * step + i, y * picks + j]
                 src = lax.shift_right_logical(block_id, blocks.bit_length() - 1)
-                part = 2 * (block_id & (blocks - 1))
-                o_ref[i * ys + y, j] = held_ref[src, pl.ds(part, 2)]
-
-
-def pick(held, ys, picks):
-    sources, parts, rows, _ = held.shape
+                first = pl.multiple_of(2 * rows * (block_id & (blocks - 1)), 2 * rows)
+                o_ref[i * ys + y, j] = held_ref[src, pl.ds(first, 2 * rows)].reshape(2, rows, HD)
+
+
+def pick(held, ys, picks, blocks):
+    sources, length, _ = held.shape
+    rows = (length - ID_ROWS) // (2 * blocks)
     step = 8
     return pl.pallas_call(
-        functools.partial(pick_kernel, step=step, ys=ys, picks=picks),
+        functools.partial(pick_kernel, step=step, ys=ys, picks=picks, blocks=blocks, rows=rows),
         grid=(sources // step,),
         in_specs=[pl.BlockSpec(memory_space=pltpu.VMEM)],
         out_specs=pl.BlockSpec((step * ys, picks, 2, rows, HD), lambda i: (i, 0, 0, 0, 0)),
@@ -270,7 +271,7 @@
     near = near_part(core.reshape(1), queries, new_keys, new_values, their_keys, their_values)
     held, (acc, stat) = lax.optimization_barrier((held, near))
 
-    got = lax.all_to_all(pick(held, ys, picks), ("ctx", "y"), split_axis=0, concat_axis=0, tiled=True)
+    got = lax.all_to_all(pick(held, ys, picks, cache_keys.shape[0] // BLK), ("ctx", "y"), split_axis=0, concat_axis=0, tiled=True)
     other = lax.ppermute(got, "core", swap)
     split = (ctx_size, ys) + got.shape[1:]
     out = far_part(core.reshape(1), queries, got.reshape(split), acc, stat, None)

time: 173 us -> 172 us (level)
  no operation moved by 1% of the time
where the time goes in v4:
time: 172 us; the launch traced here: 171 us
  blocking collectives  80.9 us (47%)
  Pallas kernels  39 us (23%)
  waiting for transfers between devices  32.7 us (19%)
  starting transfers between devices  18.7 us (11%)
    all_to_all x1, blocking collectives, local(): lax.all_to_all(pick(held, ys, picks, cache_keys.shape[0] // BLK), ('ctx',...  80.9 us
    all_to_all x1, waiting for transfers between devices, local(): lax.all_to_all(outgoing, 'ctx', split_axis=0, concat_axis=0, tiled=True)  30.4 us
    pallas_call x2, Pallas kernels, far_part(): pl.pallas_call(functools.partial(far_kernel, group=strip // HD), grid_spe...  18.6 us
    pallas_call x1, Pallas kernels, near_part(): pl.pallas_call(functools.partial(near_kernel, group=group), grid_spec=plt...  16 us
    all_to_all x1, starting transfers between devices, local(): lax.all_to_all(outgoing, 'ctx', split_axis=0, concat_axis=0, tiled=True)  12 us
    ppermute x1, starting transfers between devices, local(): other = lax.ppermute(got, 'core', swap)  5.59 us
  transfers between devices with their start and end apart: 4, of which 3 were waited for; matrix products, arithmetic and copies ran while one was open for 0% of the time, Pallas kernels for 15%

profile of v4, /device:TPU:1, one launch (start us, length us, event | category | flops | bytes accessed | tf_op | source)
XLA Modules:
  0.0 171.4 jit_solution(757720390103147917)
XLA Ops:
  0.0 2.5 %spread.1 = bf16[32,264,128]{2,1,0:T(8,128)(2,1)} custom-call(s32[3,1,4]{2,1,0:T(1,128)} %bitcast.10, bf16[8,32,16,128]{3,2,1,0:T(8,128)(2,1)} %bitcast.8, bf16[8,32,16,128]{3,2,1,0:T(8,128)(2,1)} %bitcast.9), custom_call_target="tpu_custom_call" | custom-call | tf_op jit(solution)/shard_map/spread/pallas_call | solution.py:69
  2.5 0.0 copy-start
  2.5 0.0 copy-start.1
  2.6 12.0 %all-to-all-start = ((bf16[32,264,128]{2,1,0:T(8,128)(2,1)}), bf16[32,264,128]{2,1,0:T(8,128)(2,1)S(1)}, u32[]{:S(2)}, u32[]{:S(2)}) async-start(bf16[32,264,128]{2,1,0:T(8,128)(2,1)} %spread.1), calls=%async_computation | async-start | bytes 4325376 | tf_op jit(solution)/shard_map/all_to_all | solution.py:266
  14.6 0.0 copy-done
  14.6 1.0 collective-permute-start
  15.6 0.0 copy-done.1
  15.6 0.1 collective-permute-start.1
  15.7 1.6 collective-permute-done.k2_ref
  17.3 0.7 collective-permute-done.1.v2_ref
  18.0 16.0 %near.1 = (f32[8,512,256]{2,1,0:T(8,128)}, f32[8,8,256]{2,1,0:T(8,128)}) custom-call(s32[1]{0:T(128)} %bitcast.4.core_ref.parity_ref, bf16[256,4096]{1,0:T(8,128)(2,1)} %q_ref.5, bf16[256,1024]{1,0:T(8,128)(2,1)} %k_ref.1, bf16[256,1024]{1,0:T(8,128)(2,1)} %v_ref.1, bf16[256,1024]{1,0:T(8,128)(2,1)} %collective-permute-done.k2_ref, ...), custom_call_target="tpu_custom_call" | custom-call | flops 2147483648 | bytes 9437184 | tf_op jit(solution)/shard_map/near/pallas_call | solution.py:153
  34.0 30.4 %all-to-all-done.held_ref = bf16[32,264,128]{2,1,0:T(8,128)(2,1)S(1)} async-done(((bf16[32,264,128]{2,1,0:T(8,128)(2,1)}), bf16[32,264,128]{2,1,0:T(8,128)(2,1)S(1)}, u32[]{:S(2)}, u32[]{:S(2)}) %all-to-all-start) | async-done | bytes 2162720 | tf_op jit(solution)/shard_map/all_to_all | solution.py:266
  64.4 1.9 %pick.1 = bf16[128,3,2,16,128]{4,3,2,1,0:T(8,128)(2,1)S(1)} custom-call(bf16[32,264,128]{2,1,0:T(8,128)(2,1)S(1)} %all-to-all-done.held_ref), custom_call_target="tpu_custom_call" | custom-call | tf_op jit(solution)/shard_map/pick/pallas_call | solution.py:111
  66.3 80.9 %all_to_all.10 = bf16[128,3,2,16,128]{4,3,2,1,0:T(8,128)(2,1)S(1)} all-to-all(bf16[128,3,2,16,128]{4,3,2,1,0:T(8,128)(2,1)S(1)} %pick.1), channel_id=1, replica_groups=mesh['ctx'=32,'y'=4,'core'=2] {'ctx','y'}, dimensions={0} | all-to-all | bytes 6291456 | tf_op jit(solution)/shard_map/all_to_all | solution.py:274
  147.2 5.6 %collective-permute-start.2 = (bf16[128,3,2,16,128]{4,3,2,1,0:T(8,128)(2,1)S(1)}, bf16[128,3,2,16,128]{4,3,2,1,0:T(8,128)(2,1)}, u32[]{:S(2)}, u32[]{:S(2)}) collective-permute-start(bf16[128,3,2,16,128]{4,3,2,1,0:T(8,128)(2,1)S(1)} %all_to_all.10), channel_id=1, source_target_pairs={{0,1},{1,0},{2,3},{3,2},{4,5},{5,4},{6,7},{7,6},{8,9},{9,8},{10,11... | collective-permute-start | bytes 9437192 | tf_op jit(solution)/shard_map/ppermute | solution.py:275
  152.8 9.1 %far.2.rest_0_ = bf16[256,4096]{1,0:T(8,128)(2,1)} custom-call(s32[1]{0:T(128)} %bitcast.4.core_ref.parity_ref, bf16[256,4096]{1,0:T(8,128)(2,1)} %q_ref.5, bf16[32,4,3,2,16,128]{5,4,3,2,1,0:T(8,128)(2,1)S(1)} %bitcast.7, f32[8,512,256]{2,1,0:T(8,128)} %get-tuple-element.15.acc_ref, f32[8,8,256]{2,1,0:T(8,128)} %get-tuple-element.16.stat_ref), custom_call_target="tpu_custom_call" | custom-call | flops 3221225472 | bytes 7340032 | tf_op jit(solution)/shard_map/far/pallas_call | solution.py:242
  161.9 0.0 collective-permute-done.2
  161.9 9.4 %far.3 = bf16[256,4096]{1,0:T(8,128)(2,1)} custom-call(s32[1]{0:T(128)} %bitcast.parity_ref, bf16[256,4096]{1,0:T(8,128)(2,1)} %q_ref.5, bf16[32,4,3,2,16,128]{5,4,3,2,1,0:T(8,128)(2,1)} %bitcast.6.kv_ref, f32[8,512,256]{2,1,0:T(8,128)} %get-tuple-element.15.acc_ref, f32[8,8,256]{2,1,0:T(8,128)} %get-tuple-element.16.stat_ref, ...), custom_call_target="tpu_custom_call", output_to_operand_aliasing={{}: (5, {})} | custom-call | flops 3221225472 | bytes 7340032 | tf_op jit(solution)/shard_map/far/pallas_call | solution.py:242
Async XLA Ops:
  2.5 12.0 %copy-start = (bf16[256,1024]{1,0:T(8,128)(2,1)S(1)}, bf16[256,1024]{1,0:T(8,128)(2,1)}, u32[]{:S(2)}) copy-start(bf16[256,1024]{1,0:T(8,128)(2,1)} %k_ref.1) | copy-start | bytes 1572868
  2.5 13.1 %copy-start.1 = (bf16[256,1024]{1,0:T(8,128)(2,1)S(1)}, bf16[256,1024]{1,0:T(8,128)(2,1)}, u32[]{:S(2)}) copy-start(bf16[256,1024]{1,0:T(8,128)(2,1)} %v_ref.1) | copy-start | bytes 1572868
  2.6 61.8 %all-to-all-start = ((bf16[32,264,128]{2,1,0:T(8,128)(2,1)}), bf16[32,264,128]{2,1,0:T(8,128)(2,1)S(1)}, u32[]{:S(2)}, u32[]{:S(2)}) async-start(bf16[32,264,128]{2,1,0:T(8,128)(2,1)} %spread.1), calls=%async_computation | async-start | bytes 4325376 | tf_op jit(solution)/shard_map/all_to_all | solution.py:266
  14.6 2.7 %collective-permute-start = (bf16[256,1024]{1,0:T(8,128)(2,1)S(1)}, bf16[256,1024]{1,0:T(8,128)(2,1)}, u32[]{:S(2)}, u32[]{:S(2)}) collective-permute-start(bf16[256,1024]{1,0:T(8,128)(2,1)S(1)} %copy-done), channel_id=1, source_target_pairs={{0,1},{1,0},{2,3},{3,2},{4,5},{5,4},{6,7},{7,6},{8,9},{9,8},{10,11... | collective-permute-start | bytes 1572872 | tf_op jit(solution)/shard_map/ppermute | solution.py:269
  15.6 2.4 %collective-permute-start.1 = (bf16[256,1024]{1,0:T(8,128)(2,1)S(1)}, bf16[256,1024]{1,0:T(8,128)(2,1)}, u32[]{:S(2)}, u32[]{:S(2)}) collective-permute-start(bf16[256,1024]{1,0:T(8,128)(2,1)S(1)} %copy-done.1), channel_id=1, source_target_pairs={{0,1},{1,0},{2,3},{3,2},{4,5},{5,4},{6,7},{7,6},{8,9},{9,8},{10,11... | collective-permute-start | bytes 1572872 | tf_op jit(solution)/shard_map/ppermute | solution.py:270
  147.2 14.7 %collective-permute-start.2 = (bf16[128,3,2,16,128]{4,3,2,1,0:T(8,128)(2,1)S(1)}, bf16[128,3,2,16,128]{4,3,2,1,0:T(8,128)(2,1)}, u32[]{:S(2)}, u32[]{:S(2)}) collective-permute-start(bf16[128,3,2,16,128]{4,3,2,1,0:T(8,128)(2,1)S(1)} %all_to_all.10), channel_id=1, source_target_pairs={{0,1},{1,0},{2,3},{3,2},{4,5},{5,4},{6,7},{7,6},{8,9},{9,8},{10,11... | collective-permute-start | bytes 9437192 | tf_op jit(solution)/shard_map/ppermute | solution.py:275

commit v5 on v4

--- a/solution.py
+++ b/solution.py
@@ -15,6 +15,7 @@
 EXP_SCALE = math.log2(math.e) / math.sqrt(HD)
 NEG = -1e30
 ID_ROWS = 8
+FAR_HEADS = 2
 NT = (((1,), (1,)), ((), ()))
 NN = (((1,), (0,)), ((), ()))
 
@@ -84,36 +85,33 @@
     )(*(in_hbm(x) for x in (chosen.transpose(2, 1, 0), cache_keys.reshape(shape), cache_values.reshape(shape))))
 
 
-def pick_kernel(held_ref, o_ref, wide, ids, sem, *, step, ys, picks, blocks, rows):
-    at = pl.program_id(0)
-
-    @pl.when(at == 0)
-    def _():
-        tail = held_ref[:, 2 * blocks * rows :].astype(jnp.float32)
-        wide[...] = tail[:, 0, :].astype(jnp.int32)
-        copy = pltpu.make_async_copy(wide, ids, sem)
-        copy.start()
-        copy.wait()
-
-    for i in range(step):
+def pick_kernel(held_ref, o_ref, wide, ids, sem, *, ys, picks, blocks, rows):
+    tail = held_ref[:, 2 * blocks * rows :].astype(jnp.float32)
+    wide[...] = tail[:, 0, :].astype(jnp.int32)
+    copy = pltpu.make_async_copy(wide, ids, sem)
+    copy.start()
+    copy.wait()
+
+    def one(at, carry):
         for y in range(ys):
             for j in range(picks):
-                block_id = ids[at * step + i, y * picks + j]
+                block_id = ids[at, y * picks + j]
                 src = lax.shift_right_logical(block_id, blocks.bit_length() - 1)
                 first = pl.multiple_of(2 * rows * (block_id & (blocks - 1)), 2 * rows)
-                o_ref[i * ys + y, j] = held_ref[src, pl.ds(first, 2 * rows)].reshape(2, rows, HD)
+                o_ref[at * ys + y, j] = held_ref[src, pl.ds(first, 2 * rows)].reshape(2, rows, HD)
+        return carry
+
+    lax.fori_loop(0, held_ref.shape[0], one, 0, unroll=4)
 
 
 def pick(held, ys, picks, blocks):
     sources, length, _ = held.shape
     rows = (length - ID_ROWS) // (2 * blocks)
-    step = 8
     return pl.pallas_call(
-        functools.partial(pick_kernel, step=step, ys=ys, picks=picks, blocks=blocks, rows=rows),
-        grid=(sources // step,),
+        functools.partial(pick_kernel, ys=ys, picks=picks, blocks=blocks, rows=rows),
         in_specs=[pl.BlockSpec(memory_space=pltpu.VMEM)],
-        out_specs=pl.BlockSpec((step * ys, picks, 2, rows, HD), lambda i: (i, 0, 0, 0, 0)),
-        out_shape=jax.ShapeDtypeStruct((sources * ys, picks, 2, rows, HD), held.dtype),
+        out_specs=pl.BlockSpec(memory_space=pltpu.VMEM),
+        out_shape=pltpu.VMEM((sources * ys, picks, 2, rows, HD), held.dtype),
         scratch_shapes=[
             pltpu.VMEM((sources, HD), jnp.int32),
             pltpu.SMEM((sources, HD), jnp.int32),
@@ -173,76 +171,104 @@
     )(core, *(in_hbm(x) for x in (queries, keys, values, their_keys, their_values)))
 
 
-def far_kernel(parity_ref, q_ref, kv_ref, acc_ref, stat_ref, *rest, group):
-    o_ref = rest[-1]
+def far_kernel(parity_ref, *refs, heads, group, per, ys):
+    q_refs, (kv_ref, acc_ref, stat_ref, *_, o_hbm, done, sems) = refs[:heads], refs[heads:]
+    step = pl.program_id(0)
     pieces, _, picks, _, piece_rows, _ = kv_ref.shape
     far = pieces * picks * piece_rows
-    at = pl.program_id(0) if kv_ref.shape[1] > 1 else 0
-    keys = kv_ref[:, at, :, 0].reshape(far, HD)
-    values = kv_ref[:, at, :, 1].reshape(far, HD).T
-    tall = jnp.concatenate([values, jnp.ones((16, far), values.dtype)], axis=0)
+    keys, tall = [], []
+    for k in range(heads):
+        at = step * heads + k if kv_ref.shape[1] > heads else k
+        keys.append(kv_ref[:, at, :, 0].reshape(far, HD))
+        values = kv_ref[:, at, :, 1].reshape(far, HD).T
+        tall.append(jnp.concatenate([values, jnp.ones((16, far), values.dtype)], axis=0))
+    items = [(k, g) for k in range(heads) for g in range(group)]
 
     def columns(g):
         return slice(g * HD, (g + 1) * HD)
 
-    def near_top(g):
-        return stat_ref[0, 2 * g : 2 * g + 1]
-
-    def scores(g):
-        return lax.dot_general(keys, q_ref[:, columns(g)], NT, preferred_element_type=jnp.float32)
-
-    def weigh(g):
-        return jnp.exp2(scores(g) * EXP_SCALE - near_top(g) * EXP_SCALE).astype(jnp.bfloat16)
-
-    def put(g, weights, keep):
-        mixed = lax.dot_general(tall, weights, NN, preferred_element_type=jnp.float32)
-        total = mixed[HD : HD + 1] + keep * stat_ref[0, 2 * g + 1 : 2 * g + 2]
-        mixed = (mixed[:HD] + keep * acc_ref[0, columns(g)]) / total
-        o_ref[:, columns(g)] = mixed.T.astype(o_ref.dtype)
+    def near_top(k, g):
+        return stat_ref[k, 0, 2 * g : 2 * g + 1]
+
+    def scores(k, g):
+        return lax.dot_general(keys[k], q_refs[k][:, columns(g)], NT, preferred_element_type=jnp.float32)
+
+    def weigh(k, g):
+        return jnp.exp2(scores(k, g) * EXP_SCALE - near_top(k, g) * EXP_SCALE).astype(jnp.bfloat16)
+
+    def put(k, g, weights, keep):
+        mixed = lax.dot_general(tall[k], weights, NN, preferred_element_type=jnp.float32)
+        total = mixed[HD : HD + 1] + keep * stat_ref[k, 0, 2 * g + 1 : 2 * g + 2]
+        mixed = (mixed[:HD] + keep * acc_ref[k, 0, columns(g)]) / total
+        done[step * heads + k, :, columns(g)] = mixed.T.astype(done.dtype)
         return total
 
     worst = 0.0
-    ready = weigh(0)
-    for g in range(group):
+    ready = weigh(*items[0])
+    for at, item in enumerate(items):
         weights = ready
-        if g + 1 < group:
-            ready = weigh(g + 1)
-        worst = jnp.maximum(worst, put(g, weights, 1.0))
+        if at + 1 < len(items):
+            ready = weigh(*items[at + 1])
+        worst = jnp.maximum(worst, put(*item, weights, 1.0))
 
     @pl.when(jnp.logical_not(jnp.max(worst) < 2.0**100))
     def _():
-        for g in range(group):
-            raw = scores(g)
-            top = jnp.maximum(jnp.max(raw, axis=0, keepdims=True), near_top(g))
+        for item in items:
+            raw = scores(*item)
+            top = jnp.maximum(jnp.max(raw, axis=0, keepdims=True), near_top(*item))
             exact = jnp.exp2((raw - top) * EXP_SCALE).astype(jnp.bfloat16)
-            put(g, exact, jnp.exp2((near_top(g) - top) * EXP_SCALE))
+            put(*item, exact, jnp.exp2((near_top(*item) - top) * EXP_SCALE))
+
+    def out_copy(y):
+        strip = pl.ds(pl.multiple_of((per * y + parity_ref[0]) * group * HD, group * HD), group * HD)
+        return pltpu.make_async_copy(done.at[y], o_hbm.at[:, strip], sems.at[y])
+
+    for k in range(heads):
+        out_copy(step * heads + k).start()
+
+    @pl.when(step == ys // heads - 1)
+    def _():
+        for y in range(ys):
+            out_copy(y).wait()
 
 
 def far_part(parity, queries, kv, acc, stat, prior):
     rows, width = queries.shape
     pieces, ys, picks, _, piece_rows, _ = kv.shape
-    heads, strip, _ = acc.shape
-    per = heads // ys
-    columns = pl.BlockSpec((rows, strip), lambda y, parity: (0, per * y + parity[0]))
-    in_specs = [
-        columns,
-        pl.BlockSpec(memory_space=pltpu.VMEM),
-        pl.BlockSpec((1, strip, rows), lambda y, parity: (per * y + parity[0], 0, 0)),
-        pl.BlockSpec((1, stat.shape[1], rows), lambda y, parity: (per * y + parity[0], 0, 0)),
-    ]
-    operands = [parity, in_hbm(queries), pltpu.with_memory_space_constraint(kv, pltpu.VMEM), in_hbm(acc), in_hbm(stat)]
+    strip = acc.shape[1]
+    per = acc.shape[0] // ys
+    heads = FAR_HEADS
+    anywhere = pl.BlockSpec(memory_space=pl.ANY)
+
+    def column(k):
+        return pl.BlockSpec((rows, strip), lambda i, parity: (0, per * (i * heads + k) + parity[0]))
+
+    def by_head(x):
+        x = x.reshape((ys, per) + x.shape[1:])
+        return pl.BlockSpec((heads, 1) + x.shape[2:], lambda i, parity: (i, parity[0], 0, 0)), in_hbm(x)
+
+    (acc_spec, acc), (stat_spec, stat) = by_head(acc), by_head(stat)
+    if prior is None:
+        kv_spec, kv = pl.BlockSpec(memory_space=pltpu.VMEM), pltpu.with_memory_space_constraint(kv, pltpu.VMEM)
+    else:
+        kv_spec = pl.BlockSpec((pieces, heads, picks, 2, piece_rows, HD), lambda i, parity: (0, i, 0, 0, 0, 0))
+        kv = in_hbm(kv)
+    in_specs = [column(k) for k in range(heads)] + [kv_spec, acc_spec, stat_spec]
+    operands = [parity] + [in_hbm(queries)] * heads + [kv, acc, stat]
     aliases = {}
     if prior is not None:
-        in_specs[1] = pl.BlockSpec((pieces, 1, picks, 2, piece_rows, HD), lambda y, parity: (0, y, 0, 0, 0, 0))
-        in_specs.append(pl.BlockSpec(memory_space=pl.ANY))
-        operands[2] = in_hbm(kv)
+        in_specs.append(anywhere)
+        aliases = {len(operands): 0}
         operands.append(prior)
-        aliases = {5: 0}
     far = pieces * picks * piece_rows
     return pl.pallas_call(
-        functools.partial(far_kernel, group=strip // HD),
+        functools.partial(far_kernel, heads=heads, group=strip // HD, per=per, ys=ys),
         grid_spec=pltpu.PrefetchScalarGridSpec(
-            num_scalar_prefetch=1, grid=(ys,), in_specs=in_specs, out_specs=columns
+            num_scalar_prefetch=1,
+            grid=(ys // heads,),
+            in_specs=in_specs,
+            out_specs=anywhere,
+            scratch_shapes=[pltpu.VMEM((ys, rows, strip), queries.dtype), pltpu.SemaphoreType.DMA((ys,))],
         ),
         out_shape=jax.ShapeDtypeStruct((rows, width), queries.dtype),
         input_output_aliases=aliases,
@@ -251,7 +277,7 @@
             bytes_accessed=4 * rows * width + kv.size * 2,
             transcendentals=rows * far * width // HD // per,
         ),
-        compiler_params=pltpu.CompilerParams(vmem_limit_bytes=32 * MIB),
+        compiler_params=pltpu.CompilerParams(vmem_limit_bytes=40 * MIB),
         name="far",
     )(*operands)
 

time: 172 us -> 171 us (level)
  transfers between devices with their start and end apart: 4 -> 4, of which waited for: 3 -> 3; matrix products, arithmetic and copies ran while one was open for 0% -> 0% of each run, Pallas kernels for 15% -> 14%
where the time goes in v5:
time: 171 us
  blocking collectives  80.9 us (47%)
  Pallas kernels  38 us (22%)
  waiting for transfers between devices  32.7 us (19%)
  starting transfers between devices  18.7 us (11%)
    all_to_all x1, blocking collectives, local(): lax.all_to_all(pick(held, ys, picks, cache_keys.shape[0] // BLK), ('ctx',...  80.9 us
    all_to_all x1, waiting for transfers between devices, local(): lax.all_to_all(outgoing, 'ctx', split_axis=0, concat_axis=0, tiled=True)  30.4 us
    pallas_call x2, Pallas kernels, far_part(): pl.pallas_call(functools.partial(far_kernel, heads=heads, group=strip //...  17.6 us
    pallas_call x1, Pallas kernels, near_part(): pl.pallas_call(functools.partial(near_kernel, group=group), grid_spec=plt...  16 us
    all_to_all x1, starting transfers between devices, local(): lax.all_to_all(outgoing, 'ctx', split_axis=0, concat_axis=0, tiled=True)  12 us
    ppermute x1, starting transfers between devices, local(): other = lax.ppermute(got, 'core', swap)  5.59 us
  transfers between devices with their start and end apart: 4, of which 3 were waited for; matrix products, arithmetic and copies ran while one was open for 0% of the time, Pallas kernels for 14%

profile of v5, /device:TPU:1, one launch (start us, length us, event | category | flops | bytes accessed | tf_op | source)
XLA Modules:
  0.0 170.6 jit_solution(2539936196999173110)
XLA Ops:
  0.0 2.5 %spread.1 = bf16[32,264,128]{2,1,0:T(8,128)(2,1)} custom-call(s32[3,1,4]{2,1,0:T(1,128)} %bitcast.16, bf16[8,32,16,128]{3,2,1,0:T(8,128)(2,1)} %bitcast.12, bf16[8,32,16,128]{3,2,1,0:T(8,128)(2,1)} %bitcast.13), custom_call_target="tpu_custom_call" | custom-call | tf_op jit(solution)/shard_map/spread/pallas_call | solution.py:70
  2.5 0.0 copy-start
  2.5 0.0 copy-start.1
  2.6 12.0 %all-to-all-start = ((bf16[32,264,128]{2,1,0:T(8,128)(2,1)}), bf16[32,264,128]{2,1,0:T(8,128)(2,1)S(1)}, u32[]{:S(2)}, u32[]{:S(2)}) async-start(bf16[32,264,128]{2,1,0:T(8,128)(2,1)} %spread.1), calls=%async_computation | async-start | bytes 4325376 | tf_op jit(solution)/shard_map/all_to_all | solution.py:292
  14.6 0.0 copy-done
  14.6 1.0 collective-permute-start
  15.6 0.0 copy-done.1
  15.6 0.1 collective-permute-start.1
  15.7 1.6 collective-permute-done.k2_ref
  17.3 0.7 collective-permute-done.1.v2_ref
  18.0 16.0 %near.1 = (f32[8,512,256]{2,1,0:T(8,128)}, f32[8,8,256]{2,1,0:T(8,128)}) custom-call(s32[1]{0:T(128)} %bitcast.4.core_ref.parity_ref, bf16[256,4096]{1,0:T(8,128)(2,1)} %refs_1_.3, bf16[256,1024]{1,0:T(8,128)(2,1)} %k_ref.1, bf16[256,1024]{1,0:T(8,128)(2,1)} %v_ref.1, bf16[256,1024]{1,0:T(8,128)(2,1)} %collective-permute-done.k2_ref, ...), custom_call_target="tpu_custom_call" | custom-call | flops 2147483648 | bytes 9437184 | tf_op jit(solution)/shard_map/near/pallas_call | solution.py:151
  34.0 30.4 %all-to-all-done.held_ref = bf16[32,264,128]{2,1,0:T(8,128)(2,1)S(1)} async-done(((bf16[32,264,128]{2,1,0:T(8,128)(2,1)}), bf16[32,264,128]{2,1,0:T(8,128)(2,1)S(1)}, u32[]{:S(2)}, u32[]{:S(2)}) %all-to-all-start) | async-done | bytes 2162720 | tf_op jit(solution)/shard_map/all_to_all | solution.py:292
  64.4 1.9 %pick.1 = bf16[128,3,2,16,128]{4,3,2,1,0:T(8,128)(2,1)S(1)} custom-call(bf16[32,264,128]{2,1,0:T(8,128)(2,1)S(1)} %all-to-all-done.held_ref), custom_call_target="tpu_custom_call" | custom-call | tf_op jit(solution)/shard_map/pick/pallas_call | solution.py:110
  66.3 80.9 %all_to_all.10 = bf16[128,3,2,16,128]{4,3,2,1,0:T(8,128)(2,1)S(1)} all-to-all(bf16[128,3,2,16,128]{4,3,2,1,0:T(8,128)(2,1)S(1)} %pick.1), channel_id=1, replica_groups=mesh['ctx'=32,'y'=4,'core'=2] {'ctx','y'}, dimensions={0} | all-to-all | bytes 6291456 | tf_op jit(solution)/shard_map/all_to_all | solution.py:300
  147.2 5.6 %collective-permute-start.2 = (bf16[128,3,2,16,128]{4,3,2,1,0:T(8,128)(2,1)S(1)}, bf16[128,3,2,16,128]{4,3,2,1,0:T(8,128)(2,1)}, u32[]{:S(2)}, u32[]{:S(2)}) collective-permute-start(bf16[128,3,2,16,128]{4,3,2,1,0:T(8,128)(2,1)S(1)} %all_to_all.10), channel_id=1, source_target_pairs={{0,1},{1,0},{2,3},{3,2},{4,5},{5,4},{6,7},{7,6},{8,9},{9,8},{10,11... | collective-permute-start | bytes 9437192 | tf_op jit(solution)/shard_map/ppermute | solution.py:301
  152.8 8.4 %far.2.refs_5_ = bf16[256,4096]{1,0:T(8,128)(2,1)} custom-call(s32[1]{0:T(128)} %bitcast.4.core_ref.parity_ref, bf16[256,4096]{1,0:T(8,128)(2,1)} %refs_1_.3, bf16[256,4096]{1,0:T(8,128)(2,1)} %refs_1_.3, bf16[32,4,3,2,16,128]{5,4,3,2,1,0:T(8,128)(2,1)S(1)} %bitcast.9, f32[4,2,512,256]{3,2,1,0:T(8,128)} %bitcast.10, f32[4,2,8,256]{3,2,1,0:T(8,128)} %bitcast.14), custom_call_target="tpu_custom_call" | custom-call | flops 3221225472 | bytes 7340032 | tf_op jit(solution)/shard_map/far/pallas_call | solution.py:264
  161.2 0.0 collective-permute-done.2
  161.2 9.2 %far.3 = bf16[256,4096]{1,0:T(8,128)(2,1)} custom-call(s32[1]{0:T(128)} %bitcast.parity_ref, bf16[256,4096]{1,0:T(8,128)(2,1)} %refs_1_.3, bf16[256,4096]{1,0:T(8,128)(2,1)} %refs_1_.3, bf16[32,4,3,2,16,128]{5,4,3,2,1,0:T(8,128)(2,1)} %bitcast.8.refs_2_, f32[4,2,512,256]{3,2,1,0:T(8,128)} %bitcast.11, ...), custom_call_target="tpu_custom_call", output_to_operand_aliasing={{}: (6, {})} | custom-call | flops 3221225472 | bytes 7340032 | tf_op jit(solution)/shard_map/far/pallas_call | solution.py:264
Async XLA Ops:
  2.5 12.0 %copy-start = (bf16[256,1024]{1,0:T(8,128)(2,1)S(1)}, bf16[256,1024]{1,0:T(8,128)(2,1)}, u32[]{:S(2)}) copy-start(bf16[256,1024]{1,0:T(8,128)(2,1)} %k_ref.1) | copy-start | bytes 1572868
  2.5 13.1 %copy-start.1 = (bf16[256,1024]{1,0:T(8,128)(2,1)S(1)}, bf16[256,1024]{1,0:T(8,128)(2,1)}, u32[]{:S(2)}) copy-start(bf16[256,1024]{1,0:T(8,128)(2,1)} %v_ref.1) | copy-start | bytes 1572868
  2.6 61.8 %all-to-all-start = ((bf16[32,264,128]{2,1,0:T(8,128)(2,1)}), bf16[32,264,128]{2,1,0:T(8,128)(2,1)S(1)}, u32[]{:S(2)}, u32[]{:S(2)}) async-start(bf16[32,264,128]{2,1,0:T(8,128)(2,1)} %spread.1), calls=%async_computation | async-start | bytes 4325376 | tf_op jit(solution)/shard_map/all_to_all | solution.py:292
  14.6 2.7 %collective-permute-start = (bf16[256,1024]{1,0:T(8,128)(2,1)S(1)}, bf16[256,1024]{1,0:T(8,128)(2,1)}, u32[]{:S(2)}, u32[]{:S(2)}) collective-permute-start(bf16[256,1024]{1,0:T(8,128)(2,1)S(1)} %copy-done), channel_id=1, source_target_pairs={{0,1},{1,0},{2,3},{3,2},{4,5},{5,4},{6,7},{7,6},{8,9},{9,8},{10,11... | collective-permute-start | bytes 1572872 | tf_op jit(solution)/shard_map/ppermute | solution.py:295
  15.6 2.4 %collective-permute-start.1 = (bf16[256,1024]{1,0:T(8,128)(2,1)S(1)}, bf16[256,1024]{1,0:T(8,128)(2,1)}, u32[]{:S(2)}, u32[]{:S(2)}) collective-permute-start(bf16[256,1024]{1,0:T(8,128)(2,1)S(1)} %copy-done.1), channel_id=1, source_target_pairs={{0,1},{1,0},{2,3},{3,2},{4,5},{5,4},{6,7},{7,6},{8,9},{9,8},{10,11... | collective-permute-start | bytes 1572872 | tf_op jit(solution)/shard_map/ppermute | solution.py:296
  147.2 14.0 %collective-permute-start.2 = (bf16[128,3,2,16,128]{4,3,2,1,0:T(8,128)(2,1)S(1)}, bf16[128,3,2,16,128]{4,3,2,1,0:T(8,128)(2,1)}, u32[]{:S(2)}, u32[]{:S(2)}) collective-permute-start(bf16[128,3,2,16,128]{4,3,2,1,0:T(8,128)(2,1)S(1)} %all_to_all.10), channel_id=1, source_target_pairs={{0,1},{1,0},{2,3},{3,2},{4,5},{5,4},{6,7},{7,6},{8,9},{9,8},{10,11... | collective-permute-start | bytes 9437192 | tf_op jit(solution)/shard_map/ppermute | solution.py:301

commit v6 on v5

--- a/solution.py
+++ b/solution.py
@@ -98,10 +98,10 @@
                 block_id = ids[at, y * picks + j]
                 src = lax.shift_right_logical(block_id, blocks.bit_length() - 1)
                 first = pl.multiple_of(2 * rows * (block_id & (blocks - 1)), 2 * rows)
-                o_ref[at * ys + y, j] = held_ref[src, pl.ds(first, 2 * rows)].reshape(2, rows, HD)
+                o_ref[y, at, j] = held_ref[src, pl.ds(first, 2 * rows)].reshape(2, rows, HD)
         return carry
 
-    lax.fori_loop(0, held_ref.shape[0], one, 0, unroll=4)
+    lax.fori_loop(0, held_ref.shape[0], one, 0, unroll=8)
 
 
 def pick(held, ys, picks, blocks):
@@ -111,7 +111,7 @@
         functools.partial(pick_kernel, ys=ys, picks=picks, blocks=blocks, rows=rows),
         in_specs=[pl.BlockSpec(memory_space=pltpu.VMEM)],
         out_specs=pl.BlockSpec(memory_space=pltpu.VMEM),
-        out_shape=pltpu.VMEM((sources * ys, picks, 2, rows, HD), held.dtype),
+        out_shape=pltpu.VMEM((ys, sources, picks, 2, rows, HD), held.dtype),
         scratch_shapes=[
             pltpu.VMEM((sources, HD), jnp.int32),
             pltpu.SMEM((sources, HD), jnp.int32),
@@ -174,13 +174,13 @@
 def far_kernel(parity_ref, *refs, heads, group, per, ys):
     q_refs, (kv_ref, acc_ref, stat_ref, *_, o_hbm, done, sems) = refs[:heads], refs[heads:]
     step = pl.program_id(0)
-    pieces, _, picks, _, piece_rows, _ = kv_ref.shape
+    _, pieces, picks, _, piece_rows, _ = kv_ref.shape
     far = pieces * picks * piece_rows
     keys, tall = [], []
     for k in range(heads):
-        at = step * heads + k if kv_ref.shape[1] > heads else k
-        keys.append(kv_ref[:, at, :, 0].reshape(far, HD))
-        values = kv_ref[:, at, :, 1].reshape(far, HD).T
+        at = step * heads + k if kv_ref.shape[0] > heads else k
+        keys.append(kv_ref[at, :, :, 0].reshape(far, HD))
+        values = kv_ref[at, :, :, 1].reshape(far, HD).T
         tall.append(jnp.concatenate([values, jnp.ones((16, far), values.dtype)], axis=0))
     items = [(k, g) for k in range(heads) for g in range(group)]
 
@@ -234,27 +234,28 @@
 
 def far_part(parity, queries, kv, acc, stat, prior):
     rows, width = queries.shape
-    pieces, ys, picks, _, piece_rows, _ = kv.shape
+    ys, pieces, picks, _, piece_rows, _ = kv.shape
     strip = acc.shape[1]
     per = acc.shape[0] // ys
     heads = FAR_HEADS
     anywhere = pl.BlockSpec(memory_space=pl.ANY)
+    place = in_hbm if prior is None else (lambda x: x)
 
     def column(k):
         return pl.BlockSpec((rows, strip), lambda i, parity: (0, per * (i * heads + k) + parity[0]))
 
     def by_head(x):
         x = x.reshape((ys, per) + x.shape[1:])
-        return pl.BlockSpec((heads, 1) + x.shape[2:], lambda i, parity: (i, parity[0], 0, 0)), in_hbm(x)
+        return pl.BlockSpec((heads, 1) + x.shape[2:], lambda i, parity: (i, parity[0], 0, 0)), place(x)
 
     (acc_spec, acc), (stat_spec, stat) = by_head(acc), by_head(stat)
     if prior is None:
         kv_spec, kv = pl.BlockSpec(memory_space=pltpu.VMEM), pltpu.with_memory_space_constraint(kv, pltpu.VMEM)
     else:
-        kv_spec = pl.BlockSpec((pieces, heads, picks, 2, piece_rows, HD), lambda i, parity: (0, i, 0, 0, 0, 0))
+        kv_spec = pl.BlockSpec((heads, pieces, picks, 2, piece_rows, HD), lambda i, parity: (i, 0, 0, 0, 0, 0))
         kv = in_hbm(kv)
     in_specs = [column(k) for k in range(heads)] + [kv_spec, acc_spec, stat_spec]
-    operands = [parity] + [in_hbm(queries)] * heads + [kv, acc, stat]
+    operands = [parity] + [place(queries)] * heads + [kv, acc, stat]
     aliases = {}
     if prior is not None:
         in_specs.append(anywhere)
@@ -297,9 +298,11 @@
     near = near_part(core.reshape(1), queries, new_keys, new_values, their_keys, their_values)
     held, (acc, stat) = lax.optimization_barrier((held, near))
 
-    got = lax.all_to_all(pick(held, ys, picks, cache_keys.shape[0] // BLK), ("ctx", "y"), split_axis=0, concat_axis=0, tiled=True)
+    chosen_pieces = pick(held, ys, picks, cache_keys.shape[0] // BLK)
+    split = chosen_pieces.shape
+    chosen_pieces = chosen_pieces.reshape((ys * ctx_size,) + split[2:])
+    got = lax.all_to_all(chosen_pieces, ("y", "ctx"), split_axis=0, concat_axis=0, tiled=True)
     other = lax.ppermute(got, "core", swap)
-    split = (ctx_size, ys) + got.shape[1:]
     out = far_part(core.reshape(1), queries, got.reshape(split), acc, stat, None)
     other, out = lax.optimization_barrier((other, out))
     return far_part((1 - core).reshape(1), queries, other.reshape(split), acc, stat, out)

time: 171 us -> 171 us (level)
  no operation moved by 1% of the time
where the time goes in v6:
time: 171 us
  blocking collectives  82 us (48%)
  Pallas kernels  37.7 us (22%)
  waiting for transfers between devices  32.7 us (19%)
  starting transfers between devices  18 us (11%)
    all_to_all x1, blocking collectives, local(): lax.all_to_all(chosen_pieces, ('y', 'ctx'), split_axis=0, concat_axis=0,...  82 us
    all_to_all x1, waiting for transfers between devices, local(): lax.all_to_all(outgoing, 'ctx', split_axis=0, concat_axis=0, tiled=True)  30.4 us
    pallas_call x2, Pallas kernels, far_part(): pl.pallas_call(functools.partial(far_kernel, heads=heads, group=strip //...  17.3 us
    pallas_call x1, Pallas kernels, near_part(): pl.pallas_call(functools.partial(near_kernel, group=group), grid_spec=plt...  16 us
    all_to_all x1, starting transfers between devices, local(): lax.all_to_all(outgoing, 'ctx', split_axis=0, concat_axis=0, tiled=True)  12 us
    ppermute x1, starting transfers between devices, local(): other = lax.ppermute(got, 'core', swap)  4.87 us
  transfers between devices with their start and end apart: 4, of which 3 were waited for; matrix products, arithmetic and copies ran while one was open for 0% of the time, Pallas kernels for 14%

profile of v6, /device:TPU:1, one launch (start us, length us, event | category | flops | bytes accessed | tf_op | source)
XLA Modules:
  0.0 170.7 jit_solution(17673327370801382576)
XLA Ops:
  0.0 2.5 %spread.1 = bf16[32,264,128]{2,1,0:T(8,128)(2,1)} custom-call(s32[3,1,4]{2,1,0:T(1,128)} %bitcast.18, bf16[8,32,16,128]{3,2,1,0:T(8,128)(2,1)} %bitcast.16, bf16[8,32,16,128]{3,2,1,0:T(8,128)(2,1)} %bitcast.17), custom_call_target="tpu_custom_call" | custom-call | tf_op jit(solution)/shard_map/spread/pallas_call | solution.py:70
  2.5 0.0 copy-start.3
  2.6 0.0 copy-start.4
  2.6 12.0 %all-to-all-start = ((bf16[32,264,128]{2,1,0:T(8,128)(2,1)}), bf16[32,264,128]{2,1,0:T(8,128)(2,1)S(1)}, u32[]{:S(2)}, u32[]{:S(2)}) async-start(bf16[32,264,128]{2,1,0:T(8,128)(2,1)} %spread.1), calls=%async_computation | async-start | bytes 4325376 | tf_op jit(solution)/shard_map/all_to_all | solution.py:293
  14.6 0.0 copy-done.3
  14.6 1.0 collective-permute-start
  15.6 0.0 copy-done.4
  15.6 0.1 collective-permute-start.1
  15.8 1.6 collective-permute-done.k2_ref
  17.3 0.7 collective-permute-done.1.v2_ref
  18.1 16.0 %near.1 = (f32[8,512,256]{2,1,0:T(8,128)}, f32[8,8,256]{2,1,0:T(8,128)}) custom-call(s32[1]{0:T(128)} %bitcast.4.core_ref.parity_ref, bf16[256,4096]{1,0:T(8,128)(2,1)} %refs_1_.3, bf16[256,1024]{1,0:T(8,128)(2,1)} %k_ref.1, bf16[256,1024]{1,0:T(8,128)(2,1)} %v_ref.1, bf16[256,1024]{1,0:T(8,128)(2,1)} %collective-permute-done.k2_ref, ...), custom_call_target="tpu_custom_call" | custom-call | flops 2147483648 | bytes 9437184 | tf_op jit(solution)/shard_map/near/pallas_call | solution.py:151
  34.0 30.4 %all-to-all-done.held_ref = bf16[32,264,128]{2,1,0:T(8,128)(2,1)S(1)} async-done(((bf16[32,264,128]{2,1,0:T(8,128)(2,1)}), bf16[32,264,128]{2,1,0:T(8,128)(2,1)S(1)}, u32[]{:S(2)}, u32[]{:S(2)}) %all-to-all-start) | async-done | bytes 2162720 | tf_op jit(solution)/shard_map/all_to_all | solution.py:293
  64.4 1.9 %pick.1 = bf16[4,32,3,2,16,128]{5,4,3,2,1,0:T(8,128)(2,1)S(1)} custom-call(bf16[32,264,128]{2,1,0:T(8,128)(2,1)S(1)} %all-to-all-done.held_ref), custom_call_target="tpu_custom_call" | custom-call | tf_op jit(solution)/shard_map/pick/pallas_call | solution.py:110
  66.3 82.0 %all_to_all.10 = bf16[128,3,2,16,128]{4,3,2,1,0:T(8,128)(2,1)S(1)} all-to-all(bf16[128,3,2,16,128]{4,3,2,1,0:T(8,128)(2,1)S(1)} %bitcast.13), channel_id=1, replica_groups=mesh['ctx'=32,'y'=4,'core'=2] {'y','ctx'}, dimensions={0} | all-to-all | bytes 6291456 | tf_op jit(solution)/shard_map/all_to_all | solution.py:304
  148.2 4.9 %collective-permute-start.2 = (bf16[128,3,2,16,128]{4,3,2,1,0:T(8,128)(2,1)S(1)}, bf16[128,3,2,16,128]{4,3,2,1,0:T(8,128)(2,1)}, u32[]{:S(2)}, u32[]{:S(2)}) collective-permute-start(bf16[128,3,2,16,128]{4,3,2,1,0:T(8,128)(2,1)S(1)} %all_to_all.10), channel_id=1, source_target_pairs={{0,1},{1,0},{2,3},{3,2},{4,5},{5,4},{6,7},{7,6},{8,9},{9,8},{10,11... | collective-permute-start | bytes 9437192 | tf_op jit(solution)/shard_map/ppermute | solution.py:305
  153.1 0.0 copy-start
  153.1 0.0 copy-start.1
  153.1 0.0 copy-start.2
  153.1 8.6 %far.2.refs_5_ = bf16[256,4096]{1,0:T(8,128)(2,1)} custom-call(s32[1]{0:T(128)} %bitcast.4.core_ref.parity_ref, bf16[256,4096]{1,0:T(8,128)(2,1)} %refs_1_.3, bf16[256,4096]{1,0:T(8,128)(2,1)} %refs_1_.3, bf16[4,32,3,2,16,128]{5,4,3,2,1,0:T(8,128)(2,1)S(1)} %bitcast.12, f32[4,2,512,256]{3,2,1,0:T(8,128)} %bitcast.10, f32[4,2,8,256]{3,2,1,0:T(8,128)} %bitcast.14), custom_call_target="tpu_custom_call" | custom-call | flops 3221225472 | bytes 7340032 | tf_op jit(solution)/shard_map/far/pallas_call | solution.py:265
  161.7 0.0 collective-permute-done.2
  161.7 0.0 copy-done
  161.8 0.0 copy-done.1
  161.8 0.0 copy-done.2
  161.8 8.7 %far.3 = bf16[256,4096]{1,0:T(8,128)(2,1)} custom-call(s32[1]{0:T(128)} %bitcast.parity_ref, bf16[256,4096]{1,0:T(8,128)(2,1)S(1)} %copy-done, bf16[256,4096]{1,0:T(8,128)(2,1)S(1)} %copy-done, bf16[4,32,3,2,16,128]{5,4,3,2,1,0:T(8,128)(2,1)} %bitcast.9.refs_2_, f32[4,2,512,256]{3,2,1,0:T(8,128)S(1)} %bitcast.11, ...), custom_call_target="tpu_custom_call", output_to_operand_aliasing={{}: (6, {})} | custom-call | flops 3221225472 | bytes 7340032 | tf_op jit(solution)/shard_map/far/pallas_call | solution.py:265
Async XLA Ops:
  2.5 12.0 %copy-start.3 = (bf16[256,1024]{1,0:T(8,128)(2,1)S(1)}, bf16[256,1024]{1,0:T(8,128)(2,1)}, u32[]{:S(2)}) copy-start(bf16[256,1024]{1,0:T(8,128)(2,1)} %k_ref.1) | copy-start | bytes 1572868
  2.6 13.1 %copy-start.4 = (bf16[256,1024]{1,0:T(8,128)(2,1)S(1)}, bf16[256,1024]{1,0:T(8,128)(2,1)}, u32[]{:S(2)}) copy-start(bf16[256,1024]{1,0:T(8,128)(2,1)} %v_ref.1) | copy-start | bytes 1572868
  2.6 61.8 %all-to-all-start = ((bf16[32,264,128]{2,1,0:T(8,128)(2,1)}), bf16[32,264,128]{2,1,0:T(8,128)(2,1)S(1)}, u32[]{:S(2)}, u32[]{:S(2)}) async-start(bf16[32,264,128]{2,1,0:T(8,128)(2,1)} %spread.1), calls=%async_computation | async-start | bytes 4325376 | tf_op jit(solution)/shard_map/all_to_all | solution.py:293
  14.6 2.7 %collective-permute-start = (bf16[256,1024]{1,0:T(8,128)(2,1)S(1)}, bf16[256,1024]{1,0:T(8,128)(2,1)}, u32[]{:S(2)}, u32[]{:S(2)}) collective-permute-start(bf16[256,1024]{1,0:T(8,128)(2,1)S(1)} %copy-done.3), channel_id=1, source_target_pairs={{0,1},{1,0},{2,3},{3,2},{4,5},{5,4},{6,7},{7,6},{8,9},{9,8},{10,11... | collective-permute-start | bytes 1572872 | tf_op jit(solution)/shard_map/ppermute | solution.py:296
  15.6 2.4 %collective-permute-start.1 = (bf16[256,1024]{1,0:T(8,128)(2,1)S(1)}, bf16[256,1024]{1,0:T(8,128)(2,1)}, u32[]{:S(2)}, u32[]{:S(2)}) collective-permute-start(bf16[256,1024]{1,0:T(8,128)(2,1)S(1)} %copy-done.4), channel_id=1, source_target_pairs={{0,1},{1,0},{2,3},{3,2},{4,5},{5,4},{6,7},{7,6},{8,9},{9,8},{10,11... | collective-permute-start | bytes 1572872 | tf_op jit(solution)/shard_map/ppermute | solution.py:297
  148.2 13.5 %collective-permute-start.2 = (bf16[128,3,2,16,128]{4,3,2,1,0:T(8,128)(2,1)S(1)}, bf16[128,3,2,16,128]{4,3,2,1,0:T(8,128)(2,1)}, u32[]{:S(2)}, u32[]{:S(2)}) collective-permute-start(bf16[128,3,2,16,128]{4,3,2,1,0:T(8,128)(2,1)S(1)} %all_to_all.10), channel_id=1, source_target_pairs={{0,1},{1,0},{2,3},{3,2},{4,5},{5,4},{6,7},{7,6},{8,9},{9,8},{10,11... | collective-permute-start | bytes 9437192 | tf_op jit(solution)/shard_map/ppermute | solution.py:305
  153.1 8.6 %copy-start = (bf16[256,4096]{1,0:T(8,128)(2,1)S(1)}, bf16[256,4096]{1,0:T(8,128)(2,1)}, u32[]{:S(2)}) copy-start(bf16[256,4096]{1,0:T(8,128)(2,1)} %refs_1_.3) | copy-start | bytes 6291460
  153.1 8.6 %copy-start.1 = (f32[8,512,256]{2,1,0:T(8,128)S(1)}, f32[8,512,256]{2,1,0:T(8,128)}, u32[]{:S(2)}) copy-start(f32[8,512,256]{2,1,0:T(8,128)} %get-tuple-element.15) | copy-start | bytes 12582916
  153.1 8.6 %copy-start.2 = (f32[8,8,256]{2,1,0:T(8,128)S(1)}, f32[8,8,256]{2,1,0:T(8,128)}, u32[]{:S(2)}) copy-start(f32[8,8,256]{2,1,0:T(8,128)} %get-tuple-element.16) | copy-start | bytes 196612

commit v7 on v6

--- a/solution.py
+++ b/solution.py
@@ -139,7 +139,7 @@
         stat_ref[0, 2 * g + 1 : 2 * g + 2] = jnp.sum(weights, axis=0, keepdims=True)
         acc_ref[0, cols] = lax.dot_general(
             values, weights.astype(jnp.bfloat16), NN, preferred_element_type=jnp.float32
-        )
+        ).astype(acc_ref.dtype)
 
 
 def near_part(core, queries, keys, values, their_keys, their_values):
@@ -160,7 +160,7 @@
             ],
         ),
         out_shape=[
-            pltpu.HBM((heads, strip, rows), jnp.float32),
+            pltpu.HBM((heads, strip, rows), jnp.bfloat16),
             pltpu.HBM((heads, 2 * group, rows), jnp.float32),
         ],
         cost_estimate=pl.CostEstimate(
@@ -199,7 +199,7 @@
     def put(k, g, weights, keep):
         mixed = lax.dot_general(tall[k], weights, NN, preferred_element_type=jnp.float32)
         total = mixed[HD : HD + 1] + keep * stat_ref[k, 0, 2 * g + 1 : 2 * g + 2]
-        mixed = (mixed[:HD] + keep * acc_ref[k, 0, columns(g)]) / total
+        mixed = (mixed[:HD] + keep * acc_ref[k, 0, columns(g)].astype(jnp.float32)) / total
         done[step * heads + k, :, columns(g)] = mixed.T.astype(done.dtype)
         return total
 

time: 171 us -> 171 us (level)
  no operation moved by 1% of the time
where the time goes in v7:
time: 171 us
  blocking collectives  82 us (48%)
  Pallas kernels  37.5 us (22%)
  waiting for transfers between devices  32.7 us (19%)
  starting transfers between devices  18 us (11%)
    all_to_all x1, blocking collectives, local(): lax.all_to_all(chosen_pieces, ('y', 'ctx'), split_axis=0, concat_axis=0,...  82 us
    all_to_all x1, waiting for transfers between devices, local(): lax.all_to_all(outgoing, 'ctx', split_axis=0, concat_axis=0, tiled=True)  30.4 us
    pallas_call x2, Pallas kernels, far_part(): pl.pallas_call(functools.partial(far_kernel, heads=heads, group=strip //...  17.2 us
    pallas_call x1, Pallas kernels, near_part(): pl.pallas_call(functools.partial(near_kernel, group=group), grid_spec=plt...  15.9 us
    all_to_all x1, starting transfers between devices, local(): lax.all_to_all(outgoing, 'ctx', split_axis=0, concat_axis=0, tiled=True)  12 us
    ppermute x1, starting transfers between devices, local(): other = lax.ppermute(got, 'core', swap)  4.87 us
  transfers between devices with their start and end apart: 4, of which 3 were waited for; matrix products, arithmetic and copies ran while one was open for 0% of the time, Pallas kernels for 14%

profile of v7, /device:TPU:1, one launch (start us, length us, event | category | flops | bytes accessed | tf_op | source)
XLA Modules:
  0.0 170.5 jit_solution(5525700118667740469)
XLA Ops:
  0.0 2.5 %spread.1 = bf16[32,264,128]{2,1,0:T(8,128)(2,1)} custom-call(s32[3,1,4]{2,1,0:T(1,128)} %bitcast.18, bf16[8,32,16,128]{3,2,1,0:T(8,128)(2,1)} %bitcast.16, bf16[8,32,16,128]{3,2,1,0:T(8,128)(2,1)} %bitcast.17), custom_call_target="tpu_custom_call" | custom-call | tf_op jit(solution)/shard_map/spread/pallas_call | solution.py:70
  2.5 0.0 copy-start.3
  2.6 0.0 copy-start.4
  2.6 12.0 %all-to-all-start = ((bf16[32,264,128]{2,1,0:T(8,128)(2,1)}), bf16[32,264,128]{2,1,0:T(8,128)(2,1)S(1)}, u32[]{:S(2)}, u32[]{:S(2)}) async-start(bf16[32,264,128]{2,1,0:T(8,128)(2,1)} %spread.1), calls=%async_computation | async-start | bytes 4325376 | tf_op jit(solution)/shard_map/all_to_all | solution.py:293
  14.6 0.0 copy-done.3
  14.6 1.0 collective-permute-start
  15.6 0.0 copy-done.4
  15.6 0.1 collective-permute-start.1
  15.8 1.6 collective-permute-done.k2_ref
  17.3 0.7 collective-permute-done.1.v2_ref
  18.1 15.9 %near.1 = (bf16[8,512,256]{2,1,0:T(8,128)(2,1)}, f32[8,8,256]{2,1,0:T(8,128)}) custom-call(s32[1]{0:T(128)} %bitcast.4.core_ref.parity_ref, bf16[256,4096]{1,0:T(8,128)(2,1)} %refs_1_.3, bf16[256,1024]{1,0:T(8,128)(2,1)} %k_ref.1, bf16[256,1024]{1,0:T(8,128)(2,1)} %v_ref.1, bf16[256,1024]{1,0:T(8,128)(2,1)} %collective-permute-done.k2_ref, ...), custom_call_target="tpu_custom_call" | custom-call | flops 2147483648 | bytes 9437184 | tf_op jit(solution)/shard_map/near/pallas_call | solution.py:151
  34.0 30.4 %all-to-all-done.held_ref = bf16[32,264,128]{2,1,0:T(8,128)(2,1)S(1)} async-done(((bf16[32,264,128]{2,1,0:T(8,128)(2,1)}), bf16[32,264,128]{2,1,0:T(8,128)(2,1)S(1)}, u32[]{:S(2)}, u32[]{:S(2)}) %all-to-all-start) | async-done | bytes 2162720 | tf_op jit(solution)/shard_map/all_to_all | solution.py:293
  64.4 1.9 %pick.1 = bf16[4,32,3,2,16,128]{5,4,3,2,1,0:T(8,128)(2,1)S(1)} custom-call(bf16[32,264,128]{2,1,0:T(8,128)(2,1)S(1)} %all-to-all-done.held_ref), custom_call_target="tpu_custom_call" | custom-call | tf_op jit(solution)/shard_map/pick/pallas_call | solution.py:110
  66.3 82.0 %all_to_all.10 = bf16[128,3,2,16,128]{4,3,2,1,0:T(8,128)(2,1)S(1)} all-to-all(bf16[128,3,2,16,128]{4,3,2,1,0:T(8,128)(2,1)S(1)} %bitcast.10), channel_id=1, replica_groups=mesh['ctx'=32,'y'=4,'core'=2] {'y','ctx'}, dimensions={0} | all-to-all | bytes 6291456 | tf_op jit(solution)/shard_map/all_to_all | solution.py:304
  148.2 4.9 %collective-permute-start.2 = (bf16[128,3,2,16,128]{4,3,2,1,0:T(8,128)(2,1)S(1)}, bf16[128,3,2,16,128]{4,3,2,1,0:T(8,128)(2,1)}, u32[]{:S(2)}, u32[]{:S(2)}) collective-permute-start(bf16[128,3,2,16,128]{4,3,2,1,0:T(8,128)(2,1)S(1)} %all_to_all.10), channel_id=1, source_target_pairs={{0,1},{1,0},{2,3},{3,2},{4,5},{5,4},{6,7},{7,6},{8,9},{9,8},{10,11... | collective-permute-start | bytes 9437192 | tf_op jit(solution)/shard_map/ppermute | solution.py:305
  153.1 0.0 copy-start
  153.1 0.0 copy-start.1
  153.1 0.0 copy-start.2
  153.1 8.4 %far.2.refs_5_ = bf16[256,4096]{1,0:T(8,128)(2,1)} custom-call(s32[1]{0:T(128)} %bitcast.4.core_ref.parity_ref, bf16[256,4096]{1,0:T(8,128)(2,1)} %refs_1_.3, bf16[256,4096]{1,0:T(8,128)(2,1)} %refs_1_.3, bf16[4,32,3,2,16,128]{5,4,3,2,1,0:T(8,128)(2,1)S(1)} %bitcast.11, bf16[4,2,512,256]{3,2,1,0:T(8,128)(2,1)} %bitcast.12, f32[4,2,8,256]{3,2,1,0:T(8,128)} %bitcast.14), custom_call_target="tpu_custom_call" | custom-call | flops 3221225472 | bytes 7340032 | tf_op jit(solution)/shard_map/far/pallas_call | solution.py:265
  161.6 0.0 collective-permute-done.2
  161.6 0.0 copy-done
  161.6 0.0 copy-done.1
  161.6 0.0 copy-done.2
  161.6 8.8 %far.3 = bf16[256,4096]{1,0:T(8,128)(2,1)} custom-call(s32[1]{0:T(128)} %bitcast.parity_ref, bf16[256,4096]{1,0:T(8,128)(2,1)S(1)} %copy-done, bf16[256,4096]{1,0:T(8,128)(2,1)S(1)} %copy-done, bf16[4,32,3,2,16,128]{5,4,3,2,1,0:T(8,128)(2,1)} %bitcast.9.refs_2_, bf16[4,2,512,256]{3,2,1,0:T(8,128)(2,1)S(1)} %bitcast.13, ...), custom_call_target="tpu_custom_call", output_to_operand_aliasing={{}: (6, {})} | custom-call | flops 3221225472 | bytes 7340032 | tf_op jit(solution)/shard_map/far/pallas_call | solution.py:265
Async XLA Ops:
  2.5 12.0 %copy-start.3 = (bf16[256,1024]{1,0:T(8,128)(2,1)S(1)}, bf16[256,1024]{1,0:T(8,128)(2,1)}, u32[]{:S(2)}) copy-start(bf16[256,1024]{1,0:T(8,128)(2,1)} %k_ref.1) | copy-start | bytes 1572868
  2.6 13.1 %copy-start.4 = (bf16[256,1024]{1,0:T(8,128)(2,1)S(1)}, bf16[256,1024]{1,0:T(8,128)(2,1)}, u32[]{:S(2)}) copy-start(bf16[256,1024]{1,0:T(8,128)(2,1)} %v_ref.1) | copy-start | bytes 1572868
  2.6 61.8 %all-to-all-start = ((bf16[32,264,128]{2,1,0:T(8,128)(2,1)}), bf16[32,264,128]{2,1,0:T(8,128)(2,1)S(1)}, u32[]{:S(2)}, u32[]{:S(2)}) async-start(bf16[32,264,128]{2,1,0:T(8,128)(2,1)} %spread.1), calls=%async_computation | async-start | bytes 4325376 | tf_op jit(solution)/shard_map/all_to_all | solution.py:293
  14.6 2.7 %collective-permute-start = (bf16[256,1024]{1,0:T(8,128)(2,1)S(1)}, bf16[256,1024]{1,0:T(8,128)(2,1)}, u32[]{:S(2)}, u32[]{:S(2)}) collective-permute-start(bf16[256,1024]{1,0:T(8,128)(2,1)S(1)} %copy-done.3), channel_id=1, source_target_pairs={{0,1},{1,0},{2,3},{3,2},{4,5},{5,4},{6,7},{7,6},{8,9},{9,8},{10,11... | collective-permute-start | bytes 1572872 | tf_op jit(solution)/shard_map/ppermute | solution.py:296
  15.6 2.4 %collective-permute-start.1 = (bf16[256,1024]{1,0:T(8,128)(2,1)S(1)}, bf16[256,1024]{1,0:T(8,128)(2,1)}, u32[]{:S(2)}, u32[]{:S(2)}) collective-permute-start(bf16[256,1024]{1,0:T(8,128)(2,1)S(1)} %copy-done.4), channel_id=1, source_target_pairs={{0,1},{1,0},{2,3},{3,2},{4,5},{5,4},{6,7},{7,6},{8,9},{9,8},{10,11... | collective-permute-start | bytes 1572872 | tf_op jit(solution)/shard_map/ppermute | solution.py:297
  148.2 13.3 %collective-permute-start.2 = (bf16[128,3,2,16,128]{4,3,2,1,0:T(8,128)(2,1)S(1)}, bf16[128,3,2,16,128]{4,3,2,1,0:T(8,128)(2,1)}, u32[]{:S(2)}, u32[]{:S(2)}) collective-permute-start(bf16[128,3,2,16,128]{4,3,2,1,0:T(8,128)(2,1)S(1)} %all_to_all.10), channel_id=1, source_target_pairs={{0,1},{1,0},{2,3},{3,2},{4,5},{5,4},{6,7},{7,6},{8,9},{9,8},{10,11... | collective-permute-start | bytes 9437192 | tf_op jit(solution)/shard_map/ppermute | solution.py:305
  153.1 8.5 %copy-start = (bf16[256,4096]{1,0:T(8,128)(2,1)S(1)}, bf16[256,4096]{1,0:T(8,128)(2,1)}, u32[]{:S(2)}) copy-start(bf16[256,4096]{1,0:T(8,128)(2,1)} %refs_1_.3) | copy-start | bytes 6291460
  153.1 8.5 %copy-start.1 = (bf16[8,512,256]{2,1,0:T(8,128)(2,1)S(1)}, bf16[8,512,256]{2,1,0:T(8,128)(2,1)}, u32[]{:S(2)}) copy-start(bf16[8,512,256]{2,1,0:T(8,128)(2,1)} %get-tuple-element.15) | copy-start | bytes 6291460
  153.1 8.5 %copy-start.2 = (f32[8,8,256]{2,1,0:T(8,128)S(1)}, f32[8,8,256]{2,1,0:T(8,128)}, u32[]{:S(2)}) copy-start(f32[8,8,256]{2,1,0:T(8,128)} %get-tuple-element.16) | copy-start | bytes 196612
